TPU v7x, 32 devices: a whole 2x2x4 slice. The times are simulated.
32 devices in a mesh: expert: 16 (over z, y, x), tensor: 2 (over core).
Axes of the slice: x: 2, y: 2, z: 4, core: 2. Of those that a mesh axis runs over, the one named last changes fastest.
Arguments:
- inputs: bfloat16 [4096, 2048], P(('expert', 'tensor')), may hold values from -6 to 6
- norm_attn: float32 [2048], replicated, may hold values from 0.5 to 1.5
- w_query: bfloat16 [2048, 3072], P(None, 'tensor'), may hold values from -0.125 to 0.125
- w_latent: bfloat16 [2048, 576], replicated, may hold values from -0.125 to 0.125
- norm_latent: float32 [512], replicated, may hold values from 0.5 to 1.5
- w_expand: bfloat16 [512, 4096], P(None, 'tensor'), may hold values from -0.25 to 0.25
- w_output: bfloat16 [2048, 2048], P(None, 'tensor'), may hold values from -1 to 1
- norm_moe: float32 [2048], replicated, may hold values from 0.5 to 1.5
- w_router: bfloat16 [2048, 32], replicated, may hold values from -0.0625 to 0.0625
- w_shared_gate: bfloat16 [2048, 2816], P(None, 'tensor'), may hold values from -0.125 to 0.125
- w_shared_up: bfloat16 [2048, 2816], P(None, 'tensor'), may hold values from -0.125 to 0.125
- w_shared_down: bfloat16 [2048, 2816], P(None, 'tensor'), may hold values from -0.21875 to 0.21875
- w_expert_gate: bfloat16 [32, 2048, 1408], P('expert', None, 'tensor'), may hold values from -0.125 to 0.125
- w_expert_up: bfloat16 [32, 2048, 1408], P('expert', None, 'tensor'), may hold values from -0.125 to 0.125
- w_expert_down: bfloat16 [32, 2048, 1408], P('expert', None, 'tensor'), may hold values from -0.3125 to 0.3125
- routes: int32 [4096, 6], P(('expert', 'tensor')), may hold values from 0 to 31, all different within a row; in each aligned block of 128 rows (0 to 127, 128 to 255, ...) at most 32 rows name the same one
- cotangent: bfloat16 [4096, 2048], P(('expert', 'tensor')), may hold values from -6 to 6
Outputs:
- output: bfloat16 [4096, 2048], P(('expert', 'tensor'))
- grad_inputs: float32 [4096, 2048], P(('expert', 'tensor'))
- grad_norm_attn: float32 [2048], P(('expert', 'tensor'))
- grad_query: float32 [2048, 3072], P('expert', 'tensor')
- grad_latent: float32 [2048, 576], P(('expert', 'tensor'))
- grad_norm_latent: float32 [512], P(('expert', 'tensor'))
- grad_expand: float32 [512, 4096], P('expert', 'tensor')
- grad_output: float32 [2048, 2048], P('expert', 'tensor')
- grad_norm_moe: float32 [2048], P(('expert', 'tensor'))
- grad_router: float32 [2048, 32], P(('expert', 'tensor'))
- grad_shared_gate: float32 [2048, 2816], P('expert', 'tensor')
- grad_shared_up: float32 [2048, 2816], P('expert', 'tensor')
- grad_shared_down: float32 [2048, 2816], P('expert', 'tensor')
- grad_expert_gate: float32 [32, 2048, 1408], P('expert', None, 'tensor')
- grad_expert_up: float32 [32, 2048, 1408], P('expert', None, 'tensor')
- grad_expert_down: float32 [32, 2048, 1408], P('expert', None, 'tensor')
Inputs may be any that keep to these rules, and one draw needn't show every extreme that they name: `routes`: each row names 6 different experts; among the 128 rows of one device no expert is named by more than 32 rows, and in every draw some expert is named by exactly 32 rows of some device.
All inputs are finite; a program needn't handle non-finite values.
Results may differ from a plain program's by a relative error of at most 0.025.
Values may be sent and summed in bfloat16 or wider, within the bound.
A program may use at most 320 MiB of HBM per device.

v0:
```python
import math

import jax
import jax.numpy as jnp
from jax import lax
from jax.sharding import PartitionSpec as P

NOPE = 128
ROPE = 64
VD = 128
LATENT = 512
TOPK = 6


EPS = 1e-06


def rope_tables(positions, width):
    half = width // 2
    freq = 10000.0 ** (-(jnp.arange(half, dtype=jnp.float32) * 2.0) / width)
    angle = positions.astype(jnp.float32)[:, None] * freq[None, :]
    return (jnp.cos(angle), jnp.sin(angle))


def rotate(values, cosine, sine):
    half = values.shape[-1] // 2
    first = values[..., :half]
    second = values[..., half:]
    return jnp.concatenate(
        [first * cosine - second * sine, first * sine + second * cosine], axis=-1
    )


def unrotate(grads, cosine, sine):
    half = grads.shape[-1] // 2
    first = grads[..., :half]
    second = grads[..., half:]
    return jnp.concatenate(
        [first * cosine + second * sine, second * cosine - first * sine], axis=-1
    )


def norm_back(grad_out, normed, scale, gain):
    scaled = grad_out * gain
    grad_in = scale * (scaled - normed * jnp.mean(scaled * normed, axis=-1, keepdims=True))
    return (grad_in, jnp.sum(grad_out * normed, axis=0))


def masked_scores(rows_query, key_full, first_row, scale):
    block = rows_query.shape[0]
    scores = (
        jnp.einsum("qhd,khd->hqk", rows_query, key_full, preferred_element_type=jnp.float32) * scale
    )
    allowed = (first_row + jnp.arange(block))[:, None] >= jnp.arange(key_full.shape[0])[None, :]
    return jnp.where(allowed[None], scores, -1e30)


def attention_forward(query, key_full, value, scale):
    seq_rows = query.shape[0]
    block = min(seq_rows, 512)

    def one_block(index):
        first_row = index * block
        scores = masked_scores(query, key_full, first_row, scale)
        peak = jnp.max(scores, axis=-1, keepdims=True)
        weights = jnp.exp(scores - peak)
        total = jnp.sum(weights, axis=-1, keepdims=True)
        probs = (weights / total).astype(jnp.bfloat16)
        result = jnp.einsum("hqk,khd->qhd", probs, value, preferred_element_type=jnp.float32)
        return (result.astype(jnp.bfloat16), (peak + jnp.log(total))[..., 0])

    results, log_totals = lax.map(one_block, jnp.arange(seq_rows // block))
    return (results.reshape(seq_rows, query.shape[1], value.shape[2]), log_totals)


def attention_backward(query, key_full, value, grad_attended, log_totals, scale):
    seq_rows = query.shape[0]
    block = min(seq_rows, 512)

    def one_block(carry, index):
        grad_key, grad_value = carry
        first_row = index * block
        scores = masked_scores(query, key_full, first_row, scale)
        probs = jnp.exp(scores - log_totals[index][..., None])
        grad_probs = jnp.einsum(
            "qhv,khv->hqk", grad_attended, value, preferred_element_type=jnp.float32
        )
        centre = jnp.sum(probs * grad_probs, axis=-1, keepdims=True)
        grad_scores = (probs * (grad_probs - centre)).astype(jnp.bfloat16)
        grad_rows = (
            jnp.einsum("hqk,khd->qhd", grad_scores, key_full, preferred_element_type=jnp.float32)
            * scale
        )
        grad_key = (
            grad_key
            + jnp.einsum("hqk,qhd->khd", grad_scores, query, preferred_element_type=jnp.float32)
            * scale
        )
        grad_value = grad_value + jnp.einsum(
            "hqk,qhv->khv",
            probs.astype(jnp.bfloat16),
            grad_attended,
            preferred_element_type=jnp.float32,
        )
        return ((grad_key, grad_value), grad_rows)

    start_key = jnp.zeros(key_full.shape, jnp.float32)
    start_value = jnp.zeros(value.shape, jnp.float32)
    (grad_key, grad_value), grad_query = lax.scan(
        one_block, (start_key, start_value), jnp.arange(seq_rows // block)
    )
    return (grad_query.reshape(query.shape), grad_key, grad_value)


def to_experts(grid, rows):
    gathered, rows_all = (
        lax.all_gather(grid, "tensor", axis=0, tiled=True),
        lax.all_gather(rows, "tensor", axis=0, tiled=True),
    )
    received = lax.all_to_all(gathered, "expert", split_axis=1, concat_axis=1, tiled=True)
    return (received, rows_all)


def from_experts(expert_part, shared_part):
    returned = lax.all_to_all(expert_part, "expert", split_axis=1, concat_axis=1, tiled=True)
    summed, shared_sum = (
        lax.psum_scatter(returned, "tensor", scatter_dimension=0, tiled=True).astype(jnp.float32),
        lax.psum_scatter(shared_part, "tensor", scatter_dimension=0, tiled=True).astype(
            jnp.float32
        ),
    )
    return (summed, shared_sum)


def per_device(
    inputs,
    norm_attn,
    w_query,
    w_latent,
    norm_latent,
    w_expand,
    w_output,
    norm_moe,
    w_router,
    w_shared_gate,
    w_shared_up,
    w_shared_down,
    w_expert_gate,
    w_expert_up,
    w_expert_down,
    routes,
    cotangent,
):
    own_rows = inputs.shape[0]
    width = inputs.shape[1]
    tensor_size = lax.axis_size("tensor")
    expert_size = lax.axis_size("expert")
    tensor_index = lax.axis_index("tensor")
    seq_rows = own_rows * tensor_size
    local_heads = w_query.shape[1] // (NOPE + ROPE)
    experts = w_router.shape[1]
    local_experts = experts // expert_size
    capacity = own_rows * TOPK * 4 // (3 * experts)
    scale = 1.0 / math.sqrt(NOPE + ROPE)
    flat_in = inputs.astype(jnp.float32)
    scale_one = lax.rsqrt(jnp.mean(flat_in * flat_in, axis=-1, keepdims=True) + EPS)
    normed_one = flat_in * scale_one
    h_own = (normed_one * norm_attn).astype(jnp.bfloat16)
    compressed = jnp.dot(h_own, w_latent, preferred_element_type=jnp.float32)
    lat_raw = compressed[:, :LATENT]
    scale_lat = lax.rsqrt(jnp.mean(lat_raw * lat_raw, axis=-1, keepdims=True) + EPS)
    normed_lat = lat_raw * scale_lat
    lat_own = (normed_lat * norm_latent).astype(jnp.bfloat16)
    cos_own, sin_own = rope_tables(tensor_index * own_rows + jnp.arange(own_rows), ROPE)
    rope_own = rotate(compressed[:, LATENT:], cos_own, sin_own).astype(jnp.bfloat16)
    h_all, lat_all, rope_all = (
        lax.all_gather(h_own, "tensor", axis=0, tiled=True),
        lax.all_gather(lat_own, "tensor", axis=0, tiled=True),
        lax.all_gather(rope_own, "tensor", axis=0, tiled=True),
    )
    cos_all, sin_all = rope_tables(jnp.arange(seq_rows), ROPE)
    cos_all = cos_all[:, None, :]
    sin_all = sin_all[:, None, :]
    query_raw = jnp.dot(h_all, w_query, preferred_element_type=jnp.float32).reshape(
        seq_rows, local_heads, NOPE + ROPE
    )
    query = jnp.concatenate(
        [query_raw[..., :NOPE], rotate(query_raw[..., NOPE:], cos_all, sin_all)], axis=-1
    ).astype(jnp.bfloat16)
    expanded = jnp.dot(lat_all, w_expand, preferred_element_type=jnp.float32).astype(jnp.bfloat16)
    expanded = expanded.reshape(seq_rows, local_heads, NOPE + VD)
    key_full = jnp.concatenate(
        [
            expanded[..., :NOPE],
            jnp.broadcast_to(rope_all[:, None, :], (seq_rows, local_heads, ROPE)),
        ],
        axis=-1,
    )
    value = expanded[..., NOPE:]
    attended, log_totals = attention_forward(query, key_full, value, scale)
    attended_flat = attended.reshape(seq_rows, local_heads * VD)
    attn_terms = jnp.einsum(
        "sv,dv->sd", attended_flat, w_output, preferred_element_type=jnp.float32
    )
    after_attn = flat_in + lax.psum_scatter(
        attn_terms.astype(jnp.bfloat16), "tensor", scatter_dimension=0, tiled=True
    ).astype(jnp.float32)
    scale_two = lax.rsqrt(jnp.mean(after_attn * after_attn, axis=-1, keepdims=True) + EPS)
    normed_two = after_attn * scale_two
    h_moe = (normed_two * norm_moe).astype(jnp.bfloat16)
    logits = jnp.dot(h_moe, w_router, preferred_element_type=jnp.float32)
    expert_ids = jnp.arange(experts, dtype=jnp.int32)
    route_hot = (routes[:, :, None] == expert_ids[None, None, :]).astype(jnp.float32)
    gates = jax.nn.softmax(jnp.sum(route_hot * logits[:, None, :], axis=-1), axis=-1)
    flat_routes = routes.reshape(-1)
    pair_hot = (flat_routes[:, None] == expert_ids[None, :]).astype(jnp.int32)
    earlier = jnp.cumsum(pair_hot, axis=0, dtype=jnp.int32) - pair_hot
    slots = jnp.sum(earlier * pair_hot, axis=1, dtype=jnp.int32) * experts + flat_routes
    grid_shape = (capacity, expert_size, local_experts, width)

    def to_slots(pair_rows):
        placed = jnp.zeros((capacity * experts, width), jnp.bfloat16).at[slots].set(pair_rows)
        return placed.reshape(grid_shape)

    def from_slots(grid):
        return grid.reshape(capacity * experts, width)[slots].reshape(own_rows, TOPK, width)

    received, h_moe_all = to_experts(to_slots(jnp.repeat(h_moe, TOPK, axis=0)), h_moe)
    gate_act = jnp.einsum(
        "cnjd,jdf->cnjf", received, w_expert_gate, preferred_element_type=jnp.float32
    )
    up_act = jnp.einsum("cnjd,jdf->cnjf", received, w_expert_up, preferred_element_type=jnp.float32)
    hidden = (jax.nn.silu(gate_act) * up_act).astype(jnp.bfloat16)
    expert_part = jnp.einsum(
        "cnjf,jdf->cnjd", hidden, w_expert_down, preferred_element_type=jnp.float32
    ).astype(jnp.bfloat16)
    shared_gate_act = jnp.dot(h_moe_all, w_shared_gate, preferred_element_type=jnp.float32)
    shared_up_act = jnp.dot(h_moe_all, w_shared_up, preferred_element_type=jnp.float32)
    shared_hidden = (jax.nn.silu(shared_gate_act) * shared_up_act).astype(jnp.bfloat16)
    shared_part = jnp.einsum(
        "sf,df->sd", shared_hidden, w_shared_down, preferred_element_type=jnp.float32
    ).astype(jnp.bfloat16)
    expert_out, shared_out = from_experts(expert_part, shared_part)
    picked = from_slots(expert_out)
    output = (after_attn + jnp.sum(gates[:, :, None] * picked, axis=1) + shared_out).astype(
        jnp.bfloat16
    )
    grad_out = cotangent.astype(jnp.float32)
    grad_gates = jnp.sum(picked * grad_out[:, None, :], axis=-1)
    grad_select = gates * (grad_gates - jnp.sum(gates * grad_gates, axis=-1, keepdims=True))
    grad_logits = jnp.sum(grad_select[:, :, None] * route_hot, axis=1).astype(jnp.bfloat16)
    grad_router = jnp.einsum("td,te->de", h_moe, grad_logits, preferred_element_type=jnp.float32)
    pair_grads = (
        (gates[:, :, None] * grad_out[:, None, :])
        .astype(jnp.bfloat16)
        .reshape(own_rows * TOPK, width)
    )
    grad_received, cot_all = to_experts(to_slots(pair_grads), cotangent)
    grad_hidden = jnp.einsum(
        "cnjd,jdf->cnjf", grad_received, w_expert_down, preferred_element_type=jnp.float32
    )
    sigma = jax.nn.sigmoid(gate_act)
    grad_up = (grad_hidden * gate_act * sigma).astype(jnp.bfloat16)
    grad_gate = (grad_hidden * up_act * sigma * (1.0 + gate_act * (1.0 - sigma))).astype(
        jnp.bfloat16
    )
    grad_expert_down = jnp.einsum(
        "cnjd,cnjf->jdf", grad_received, hidden, preferred_element_type=jnp.float32
    )
    grad_expert_gate = jnp.einsum(
        "cnjd,cnjf->jdf", received, grad_gate, preferred_element_type=jnp.float32
    )
    grad_expert_up = jnp.einsum(
        "cnjd,cnjf->jdf", received, grad_up, preferred_element_type=jnp.float32
    )
    grad_rows_part = (
        jnp.einsum("cnjf,jdf->cnjd", grad_gate, w_expert_gate, preferred_element_type=jnp.float32)
        + jnp.einsum("cnjf,jdf->cnjd", grad_up, w_expert_up, preferred_element_type=jnp.float32)
    ).astype(jnp.bfloat16)
    shared_grad_hidden = jnp.einsum(
        "sd,df->sf", cot_all, w_shared_down, preferred_element_type=jnp.float32
    )
    shared_sigma = jax.nn.sigmoid(shared_gate_act)
    shared_grad_up = (shared_grad_hidden * shared_gate_act * shared_sigma).astype(jnp.bfloat16)
    shared_grad_gate = (
        shared_grad_hidden
        * shared_up_act
        * shared_sigma
        * (1.0 + shared_gate_act * (1.0 - shared_sigma))
    ).astype(jnp.bfloat16)
    grad_shared_down = jnp.einsum(
        "sd,sf->df", cot_all, shared_hidden, preferred_element_type=jnp.float32
    )
    grad_shared_gate = jnp.einsum(
        "sd,sf->df", h_moe_all, shared_grad_gate, preferred_element_type=jnp.float32
    )
    grad_shared_up = jnp.einsum(
        "sd,sf->df", h_moe_all, shared_grad_up, preferred_element_type=jnp.float32
    )
    shared_rows_part = (
        jnp.einsum("sf,df->sd", shared_grad_gate, w_shared_gate, preferred_element_type=jnp.float32)
        + jnp.einsum("sf,df->sd", shared_grad_up, w_shared_up, preferred_element_type=jnp.float32)
    ).astype(jnp.bfloat16)
    grad_rows, grad_shared_rows = from_experts(grad_rows_part, shared_rows_part)
    grad_moe = (
        jnp.sum(from_slots(grad_rows), axis=1)
        + grad_shared_rows
        + jnp.einsum("te,de->td", grad_logits, w_router, preferred_element_type=jnp.float32)
    )
    grad_mid, grad_norm_moe = norm_back(grad_moe, normed_two, scale_two, norm_moe)
    grad_mid = grad_mid + grad_out
    grad_attn = grad_mid.astype(jnp.bfloat16)
    grad_attn_all = lax.all_gather(grad_attn, "tensor", axis=0, tiled=True)
    grad_output = jnp.einsum(
        "sd,sv->dv", grad_attn_all, attended_flat, preferred_element_type=jnp.float32
    )
    grad_attended = jnp.einsum(
        "sd,dv->sv", grad_attn_all, w_output, preferred_element_type=jnp.float32
    )
    grad_attended = grad_attended.astype(jnp.bfloat16).reshape(seq_rows, local_heads, VD)
    grad_query_full, grad_key_full, grad_value = attention_backward(
        query, key_full, value, grad_attended, log_totals, scale
    )
    grad_query_raw = jnp.concatenate(
        [grad_query_full[..., :NOPE], unrotate(grad_query_full[..., NOPE:], cos_all, sin_all)],
        axis=-1,
    )
    grad_query_raw = grad_query_raw.astype(jnp.bfloat16).reshape(
        seq_rows, local_heads * (NOPE + ROPE)
    )
    grad_query = jnp.einsum("sd,sq->dq", h_all, grad_query_raw, preferred_element_type=jnp.float32)
    grad_expanded = jnp.concatenate([grad_key_full[..., :NOPE], grad_value], axis=-1)
    grad_expanded = grad_expanded.astype(jnp.bfloat16).reshape(seq_rows, local_heads * (NOPE + VD))
    grad_expand = jnp.einsum(
        "sl,sk->lk", lat_all, grad_expanded, preferred_element_type=jnp.float32
    )
    grad_rope_part = jnp.sum(grad_key_full[..., NOPE:], axis=1)
    grad_h_part = jnp.einsum(
        "sq,dq->sd", grad_query_raw, w_query, preferred_element_type=jnp.float32
    )
    grad_lat_part = jnp.einsum(
        "sk,lk->sl", grad_expanded, w_expand, preferred_element_type=jnp.float32
    )
    grad_h_own, grad_lat_own, grad_rope_own = (
        lax.psum_scatter(
            grad_h_part.astype(jnp.bfloat16), "tensor", scatter_dimension=0, tiled=True
        ).astype(jnp.float32),
        lax.psum_scatter(
            grad_lat_part.astype(jnp.bfloat16), "tensor", scatter_dimension=0, tiled=True
        ).astype(jnp.float32),
        lax.psum_scatter(
            grad_rope_part.astype(jnp.bfloat16), "tensor", scatter_dimension=0, tiled=True
        ).astype(jnp.float32),
    )
    grad_lat_raw, grad_norm_latent = norm_back(grad_lat_own, normed_lat, scale_lat, norm_latent)
    grad_compressed = jnp.concatenate(
        [grad_lat_raw, unrotate(grad_rope_own, cos_own, sin_own)], axis=-1
    ).astype(jnp.bfloat16)
    grad_latent = jnp.einsum(
        "td,tc->dc", h_own, grad_compressed, preferred_element_type=jnp.float32
    )
    grad_h = grad_h_own + jnp.einsum(
        "tc,dc->td", grad_compressed, w_latent, preferred_element_type=jnp.float32
    )
    grad_in, grad_norm_attn = norm_back(grad_h, normed_one, scale_one, norm_attn)
    grad_inputs = grad_mid + grad_in
    grad_query, grad_expand, grad_output, grad_shared_gate, grad_shared_up, grad_shared_down = (
        lax.psum_scatter(
            grad_query.astype(jnp.bfloat16), "expert", scatter_dimension=0, tiled=True
        ).astype(jnp.float32),
        lax.psum_scatter(
            grad_expand.astype(jnp.bfloat16), "expert", scatter_dimension=0, tiled=True
        ).astype(jnp.float32),
        lax.psum_scatter(
            grad_output.astype(jnp.bfloat16), "expert", scatter_dimension=0, tiled=True
        ).astype(jnp.float32),
        lax.psum_scatter(
            grad_shared_gate.astype(jnp.bfloat16), "expert", scatter_dimension=0, tiled=True
        ).astype(jnp.float32),
        lax.psum_scatter(
            grad_shared_up.astype(jnp.bfloat16), "expert", scatter_dimension=0, tiled=True
        ).astype(jnp.float32),
        lax.psum_scatter(
            grad_shared_down.astype(jnp.bfloat16), "expert", scatter_dimension=0, tiled=True
        ).astype(jnp.float32),
    )
    grad_latent, grad_router, grad_norm_attn, grad_norm_moe, grad_norm_latent = (
        lax.psum_scatter(grad_latent, ("expert", "tensor"), scatter_dimension=0, tiled=True),
        lax.psum_scatter(grad_router, ("expert", "tensor"), scatter_dimension=0, tiled=True),
        lax.psum_scatter(grad_norm_attn, ("expert", "tensor"), scatter_dimension=0, tiled=True),
        lax.psum_scatter(grad_norm_moe, ("expert", "tensor"), scatter_dimension=0, tiled=True),
        lax.psum_scatter(grad_norm_latent, ("expert", "tensor"), scatter_dimension=0, tiled=True),
    )
    return (
        output,
        grad_inputs,
        grad_norm_attn,
        grad_query,
        grad_latent,
        grad_norm_latent,
        grad_expand,
        grad_output,
        grad_norm_moe,
        grad_router,
        grad_shared_gate,
        grad_shared_up,
        grad_shared_down,
        grad_expert_gate,
        grad_expert_up,
        grad_expert_down,
    )


def solution(mesh):
    return jax.shard_map(
        per_device,
        mesh=mesh,
        in_specs=(
            P(("expert", "tensor"), None),
            P(),
            P(None, "tensor"),
            P(),
            P(),
            P(None, "tensor"),
            P(None, "tensor"),
            P(),
            P(),
            P(None, "tensor"),
            P(None, "tensor"),
            P(None, "tensor"),
            P("expert", None, "tensor"),
            P("expert", None, "tensor"),
            P("expert", None, "tensor"),
            P(("expert", "tensor"), None),
            P(("expert", "tensor"), None),
        ),
        out_specs=(
            P(("expert", "tensor"), None),
            P(("expert", "tensor"), None),
            P(("expert", "tensor")),
            P("expert", "tensor"),
            P(("expert", "tensor"), None),
            P(("expert", "tensor")),
            P("expert", "tensor"),
            P("expert", "tensor"),
            P(("expert", "tensor")),
            P(("expert", "tensor"), None),
            P("expert", "tensor"),
            P("expert", "tensor"),
            P("expert", "tensor"),
            P("expert", None, "tensor"),
            P("expert", None, "tensor"),
            P("expert", None, "tensor"),
        ),
        check_vma=False,
    )
```

profile of v0, /device:TPU:0, one launch (start us, length us, event | category | flops | bytes accessed | tf_op | source)
XLA Modules:
  0.0 2232.6 jit_solution(16420816027828457943)
XLA Ops:
  84.2 21.2 all-gather.9.cloned.1.call-done
  105.4 11.4 copy.193
  138.5 14.8 scatter_custom_fusion.1
  167.0 21.3 all-gather.13.cloned.1.call-done
  188.3 11.4 copy.201
  199.7 83.3 %all-to-all-done = bf16[64,16,2,2048]{3,0,2,1:T(8,128)(2,1)} async-done(((bf16[64,16,2,2048]{3,0,2,1:T(8,128)(2,1)}), bf16[64,16,2,2048]{3,0,2,1:T(8,128)(2,1)}, u32[]{:S(2)}, u32[]{:S(2)}) %all-to-all-start) | async-done | bytes 8388640 | tf_op jit(solution)/shard_map/all_to_all | solution.py:120
  283.0 38.3 %all-to-all-start.2 = ((bf16[64,16,2,2048]{3,0,2,1:T(8,128)(2,1)}), bf16[64,16,2,2048]{3,0,2,1:T(8,128)(2,1)}, u32[]{:S(2)}, u32[]{:S(2)}) async-start(bf16[64,16,2,2048]{3,0,2,1:T(8,128)(2,1)} %copy.201), calls=%async_computation.4 | async-start | bytes 16777216 | tf_op jit(solution)/shard_map/all_to_all | solution.py:120
  321.3 14.9 fusion.3
  336.2 14.9 fusion.5
  351.1 125.2 %all-to-all-done.2 = bf16[64,16,2,2048]{3,0,2,1:T(8,128)(2,1)} async-done(((bf16[64,16,2,2048]{3,0,2,1:T(8,128)(2,1)}), bf16[64,16,2,2048]{3,0,2,1:T(8,128)(2,1)}, u32[]{:S(2)}, u32[]{:S(2)}) %all-to-all-start.2) | async-done | bytes 8388640 | tf_op jit(solution)/shard_map/all_to_all | solution.py:120
  476.3 19.6 fusion.12
  495.9 13.4 fusion.20
  509.3 14.1 fusion
  523.5 11.4 copy.203
  534.9 39.7 %all-to-all-start.3 = ((bf16[64,16,2,2048]{3,0,2,1:T(8,128)(2,1)}), bf16[64,16,2,2048]{3,0,2,1:T(8,128)(2,1)}, u32[]{:S(2)}, u32[]{:S(2)}) async-start(bf16[64,16,2,2048]{3,0,2,1:T(8,128)(2,1)} %copy.203), calls=%async_computation.5 | async-start | bytes 16777216 | tf_op jit(solution)/shard_map/all_to_all | solution.py:125
  575.8 151.0 %all-to-all-done.3 = bf16[64,16,2,2048]{3,0,2,1:T(8,128)(2,1)} async-done(((bf16[64,16,2,2048]{3,0,2,1:T(8,128)(2,1)}), bf16[64,16,2,2048]{3,0,2,1:T(8,128)(2,1)}, u32[]{:S(2)}, u32[]{:S(2)}) %all-to-all-start.3) | async-done | bytes 8388640 | tf_op jit(solution)/shard_map/all_to_all | solution.py:125
  726.7 11.4 copy.230
  738.1 12.3 copy.247
  750.9 12.0 convert_bitcast_fusion
  774.3 221.9 %all_to_all.20 = bf16[64,16,2,2048]{3,0,2,1:T(8,128)(2,1)} all-to-all(bf16[64,16,2,2048]{3,0,2,1:T(8,128)(2,1)} %copy.196), channel_id=1, replica_groups=mesh['expert'=16,'tensor'=2] {'expert'}, dimensions={1} | all-to-all | bytes 16777216 | tf_op jit(solution)/shard_map/all_to_all | solution.py:125
  996.2 11.4 copy.228
  1007.6 12.3 copy.245
  1257.6 77.6 %reduce-scatter.61.cloned.1.call-done = bf16[128,1408]{1,0:T(8,128)(2,1)} async-done(((bf16[2048,1408]{1,0:T(8,128)(2,1)}), bf16[128,1408]{1,0:T(8,128)(2,1)}) %reduce-scatter.61.cloned.1.call-update) | async-done | bytes 360464
  1339.1 126.0 %reduce-scatter.47.cloned.1.call-done = bf16[128,1408]{1,0:T(8,128)(2,1)} async-done(((bf16[2048,1408]{1,0:T(8,128)(2,1)}), bf16[128,1408]{1,0:T(8,128)(2,1)}) %reduce-scatter.47.cloned.1.call-update) | async-done | bytes 360464 | tf_op jit(solution)/shard_map/reduce_scatter | solution.py:377
  1467.0 128.0 %reduce-scatter.49.cloned.1.call-done = bf16[128,1408]{1,0:T(8,128)(2,1)} async-done(((bf16[2048,1408]{1,0:T(8,128)(2,1)}), bf16[128,1408]{1,0:T(8,128)(2,1)}) %reduce-scatter.49.cloned.1.call-update) | async-done | bytes 360464 | tf_op jit(solution)/shard_map/reduce_scatter | solution.py:380
  1596.8 12.6 convolution_bitcast_fusion
  1632.0 101.0 %reduce-scatter.59.cloned.1.call-done = f32[64,32]{1,0:T(8,128)} async-done(((f32[2048,32]{1,0:T(8,128)}), f32[64,32]{1,0:T(8,128)}) %reduce-scatter.59.cloned.1.call-update) | async-done | bytes 8208
  1743.5 41.3 %all-reduce.3 = (f32[2048]{0:T(1024)S(1)}, f32[512]{0:T(512)S(1)}, f32[2048]{0:T(1024)S(1)}) all-reduce(f32[2048]{0:T(1024)} %get-tuple-element.161, f32[512]{0:T(512)S(1)} %get-tuple-element.163, f32[2048]{0:T(1024)} %get-tuple-element.159), channel_id=10, replica_groups=mesh['expert'=16,'tensor'=2] {'expert','tensor'}, use_global_device_ids=true, to_apply=%region_32.33.clone | all-reduce | flops 4608 | bytes 36864
  1791.4 44.8 %reduce-scatter.43.cloned.1.call-done = bf16[32,2048]{1,0:T(8,128)(2,1)} async-done(((bf16[512,2048]{1,0:T(8,128)(2,1)}), bf16[32,2048]{1,0:T(8,128)(2,1)}) %reduce-scatter.43.cloned.1.call-update) | async-done | bytes 131088 | tf_op jit(solution)/shard_map/reduce_scatter | solution.py:371
  1837.8 92.9 %reduce-scatter.45.cloned.1.call-done = bf16[128,1024]{1,0:T(8,128)(2,1)} async-done(((bf16[2048,1024]{1,0:T(8,128)(2,1)}), bf16[128,1024]{1,0:T(8,128)(2,1)}) %reduce-scatter.45.cloned.1.call-update) | async-done | bytes 262160 | tf_op jit(solution)/shard_map/reduce_scatter | solution.py:374
  1932.5 148.6 %reduce-scatter.39.cloned.1.call-done = bf16[128,1536]{1,0:T(8,128)(2,1)} async-done(((bf16[2048,1536]{1,0:T(8,128)(2,1)}), bf16[128,1536]{1,0:T(8,128)(2,1)}) %reduce-scatter.39.cloned.1.call-update) | async-done | bytes 393232 | tf_op jit(solution)/shard_map/reduce_scatter | solution.py:368
  2083.0 142.6 %reduce-scatter.41.cloned.1.call-done = f32[64,576]{1,0:T(8,128)} async-done(((f32[2048,576]{1,0:T(8,128)}), f32[64,576]{1,0:T(8,128)}) %reduce-scatter.41.cloned.1.call-update) | async-done | bytes 147472 | tf_op jit(solution)/shard_map/reduce_scatter | solution.py:388
  (323 shorter events, 414.9 us)
Async XLA Ops:
  7.2 17.0 all-gather.7.cloned.1.call-start
  11.3 36.4 %reduce-scatter.31.cloned.1.call-start = ((), (), s32[]{:S(2)}) async-start(), calls=%async_computation.21 | async-start | bytes 1572864 | tf_op jit(solution)/shard_map/reduce_scatter | solution.py:205
  13.3 16.7 copy-start.11
  34.1 13.6 copy-start.3
  34.1 15.5 copy-start.36
  36.4 69.0 %all-gather.9.cloned.1.call-start = ((), (), s32[]{:S(2)}) async-start(), calls=%async_computation.22 | async-start | bytes 12582912 | tf_op jit(solution)/shard_map/all_gather | solution.py:117
  39.6 98.9 %copy-start.48 = (s32[768]{0:T(1024)}, s32[768]{0:T(1024)S(1)}, u32[]{:S(2)}) copy-start(s32[768]{0:T(1024)S(1)} %fusion.89) | copy-start | bytes 9220
  116.8 166.2 %all-to-all-start = ((bf16[64,16,2,2048]{3,0,2,1:T(8,128)(2,1)}), bf16[64,16,2,2048]{3,0,2,1:T(8,128)(2,1)}, u32[]{:S(2)}, u32[]{:S(2)}) async-start(bf16[64,16,2,2048]{3,0,2,1:T(8,128)(2,1)} %copy.193), calls=%async_computation.1 | async-start | bytes 16777216 | tf_op jit(solution)/shard_map/all_to_all | solution.py:120
  123.8 64.5 %all-gather.13.cloned.1.call-start = ((), (), s32[]{:S(2)}) async-start(), calls=%async_computation.25 | async-start | bytes 12582912 | tf_op jit(solution)/shard_map/all_gather | solution.py:117
  138.4 14.9 copy-start.23
  283.0 193.3 %all-to-all-start.2 = ((bf16[64,16,2,2048]{3,0,2,1:T(8,128)(2,1)}), bf16[64,16,2,2048]{3,0,2,1:T(8,128)(2,1)}, u32[]{:S(2)}, u32[]{:S(2)}) async-start(bf16[64,16,2,2048]{3,0,2,1:T(8,128)(2,1)} %copy.201), calls=%async_computation.4 | async-start | bytes 16777216 | tf_op jit(solution)/shard_map/all_to_all | solution.py:120
  495.9 13.4 copy-start.62
  534.9 191.8 %all-to-all-start.3 = ((bf16[64,16,2,2048]{3,0,2,1:T(8,128)(2,1)}), bf16[64,16,2,2048]{3,0,2,1:T(8,128)(2,1)}, u32[]{:S(2)}, u32[]{:S(2)}) async-start(bf16[64,16,2,2048]{3,0,2,1:T(8,128)(2,1)} %copy.203), calls=%async_computation.5 | async-start | bytes 16777216 | tf_op jit(solution)/shard_map/all_to_all | solution.py:125
  574.5 447.5 %all-gather.11.cloned.1.call-start = ((), (), s32[]{:S(2)}) async-start(), calls=%async_computation.23 | async-start | bytes 1572864 | tf_op jit(solution)/shard_map/all_gather | solution.py:118
  575.1 460.1 %all-gather.15.cloned.1.call-start = ((), (), s32[]{:S(2)}) async-start(), calls=%async_computation.26 | async-start | bytes 1572864 | tf_op jit(solution)/shard_map/all_gather | solution.py:118
  575.7 476.9 %reduce-scatter.53.cloned.1.call-start = ((), (), s32[]{:S(2)}) async-start(), calls=%async_computation.37 | async-start | bytes 12582912
  750.4 345.1 %reduce-scatter.51.cloned.1.call-start = ((), (), s32[]{:S(2)}) async-start(), calls=%async_computation.36 | async-start | bytes 12582912
  1019.9 135.5 %reduce-scatter.35.cloned.1.call-start = ((), (), s32[]{:S(2)}) async-start(), calls=%async_computation.27 | async-start | bytes 1572864 | tf_op jit(solution)/shard_map/reduce_scatter | solution.py:128
  1052.6 116.9 %all-gather.17.cloned.1.call-start = ((), (), s32[]{:S(2)}) async-start(), calls=%async_computation.28 | async-start | bytes 1572864 | tf_op jit(solution)/shard_map/all_gather | solution.py:313
  1161.6 86.8 %reduce-scatter.57.cloned.1.call-start = ((), (), s32[]{:S(2)}) async-start(), calls=%async_computation.39 | async-start | bytes 98304
  1184.8 65.2 %reduce-scatter.55.cloned.1.call-start = ((), (), s32[]{:S(2)}) async-start(), calls=%async_computation.38 | async-start | bytes 393216
  1190.2 145.0 %reduce-scatter.61.cloned.1.call-start = ((), (), s32[]{:S(2)}) async-start(), calls=%async_computation.41 | async-start | bytes 6127616
  1204.2 260.8 %reduce-scatter.47.cloned.1.call-start = ((), (), s32[]{:S(2)}) async-start(), calls=%async_computation.34 | async-start | bytes 6127616 | tf_op jit(solution)/shard_map/reduce_scatter | solution.py:377
  1210.5 384.4 %reduce-scatter.49.cloned.1.call-start = ((), (), s32[]{:S(2)}) async-start(), calls=%async_computation.35 | async-start | bytes 6127616 | tf_op jit(solution)/shard_map/reduce_scatter | solution.py:380
  1216.4 516.6 %reduce-scatter.59.cloned.1.call-start = ((), (), s32[]{:S(2)}) async-start(), calls=%async_computation.40 | async-start | bytes 1081344
  1219.4 520.7 %reduce-scatter.37.cloned.1.call-start = ((), (), s32[]{:S(2)}) async-start(), calls=%async_computation.29 | async-start | bytes 1572864 | tf_op jit(solution)/shard_map/reduce_scatter | solution.py:345
  1228.2 559.1 %reduce-scatter.33.cloned.1.call-start = ((), (), s32[]{:S(2)}) async-start(), calls=%async_computation.24 | async-start | bytes 1572864 | tf_op jit(solution)/shard_map/reduce_scatter | solution.py:128
  1234.0 602.2 %reduce-scatter.43.cloned.1.call-start = ((), (), s32[]{:S(2)}) async-start(), calls=%async_computation.32 | async-start | bytes 2228224 | tf_op jit(solution)/shard_map/reduce_scatter | solution.py:371
  1237.4 693.3 %reduce-scatter.45.cloned.1.call-start = ((), (), s32[]{:S(2)}) async-start(), calls=%async_computation.33 | async-start | bytes 4456448 | tf_op jit(solution)/shard_map/reduce_scatter | solution.py:374
  1242.3 838.8 %reduce-scatter.39.cloned.1.call-start = ((), (), s32[]{:S(2)}) async-start(), calls=%async_computation.30 | async-start | bytes 6684672 | tf_op jit(solution)/shard_map/reduce_scatter | solution.py:368
  1248.3 977.3 %reduce-scatter.41.cloned.1.call-start = ((), (), s32[]{:S(2)}) async-start(), calls=%async_computation.31 | async-start | bytes 5406720 | tf_op jit(solution)/shard_map/reduce_scatter | solution.py:388
  1632.0 155.3 %copy-start.52 = (f32[128]{0:T(128)S(1)}, f32[128]{0:T(128)}, u32[]{:S(2)}) copy-start(f32[128]{0:T(128)} %copy-done.51) | copy-start | bytes 1540
  (58 other events, 221.6 us)
Sparse Core Ops, SparseCore 0:
  11.4 11.7 all-gather.6
  36.5 11.1 reduce-scatter.30
  84.4 20.9 all-gather.8
  167.1 21.0 all-gather.12
  577.3 10.2 all-gather.10
  589.0 10.1 all-gather.14
  750.5 48.6 reduce-scatter.52
  1020.1 15.4 reduce-scatter.50
  1052.7 7.3 reduce-scatter.34
  1161.7 7.8 all-gather.16
  1184.9 8.6 reduce-scatter.56
  1196.2 8.8 reduce-scatter.54
  1208.1 127.1 reduce-scatter.60
  1338.1 126.9 reduce-scatter.46
  1467.9 126.9 reduce-scatter.48
  1597.1 135.8 reduce-scatter.58
  1735.6 4.4 reduce-scatter.36
  1742.3 9.6 reduce-scatter.32
  1754.3 81.8 reduce-scatter.42
  1838.3 92.3 reduce-scatter.44
  1936.0 145.0 reduce-scatter.38
  2083.9 141.6 reduce-scatter.40
where the time goes:
time: 2240 us; the launch traced here: 2230 us
  waiting for transfers between devices  1290 us (58%)
  local copies, waits for them, and re-layouts  272 us (12%)
  blocking collectives  267 us (12%)
  matrix products  238 us (11%)
  starting transfers between devices  87.5 us (4%)
  other arithmetic  66.3 us (3%)
    all_to_all x1, blocking collectives, from_experts(): lax.all_to_all(expert_part, 'expert', split_axis=1, concat_axis=1, tiled=...  222 us
    all_to_all x2, waiting for transfers between devices, to_experts(): lax.all_to_all(gathered, 'expert', split_axis=1, concat_axis=1, tiled=True)  209 us
    unnamed x28, waiting for transfers between devices  180 us
    all_to_all x1, waiting for transfers between devices, from_experts(): lax.all_to_all(expert_part, 'expert', split_axis=1, concat_axis=1, tiled=...  151 us
    reduce_scatter x1, waiting for transfers between devices, per_device(): lax.psum_scatter(grad_query.astype(jnp.bfloat16), 'expert', scatter_dimen...  149 us
    reduce_scatter x1, waiting for transfers between devices, per_device(): lax.psum_scatter(grad_latent, ('expert', 'tensor'), scatter_dimension=0,...  143 us
    reduce_scatter x1, waiting for transfers between devices, per_device(): lax.psum_scatter(grad_shared_up.astype(jnp.bfloat16), 'expert', scatter_d...  128 us
    reduce_scatter x1, waiting for transfers between devices, per_device(): lax.psum_scatter(grad_shared_gate.astype(jnp.bfloat16), 'expert', scatter...  126 us
  transfers between devices with their start and end apart: 25, of which 16 were waited for; matrix products, arithmetic and copies ran while one was open for 19% of the time, Pallas kernels for 0%

commit v1 on v0

--- a/solution.py
+++ b/solution.py
@@ -1,10 +1,15 @@
+import functools
 import math
 
 import jax
 import jax.numpy as jnp
 from jax import lax
+from jax.experimental import pallas as pl
+from jax.experimental.pallas import tpu as pltpu
 from jax.sharding import PartitionSpec as P
 
+EXPERT = "expert"
+TENSOR = "tensor"
 NOPE = 128
 ROPE = 64
 VD = 128
@@ -114,25 +119,25 @@
 
 def to_experts(grid, rows):
     gathered, rows_all = (
-        lax.all_gather(grid, "tensor", axis=0, tiled=True),
-        lax.all_gather(rows, "tensor", axis=0, tiled=True),
-    )
-    received = lax.all_to_all(gathered, "expert", split_axis=1, concat_axis=1, tiled=True)
+        lax.all_gather(grid, TENSOR, axis=0, tiled=True),
+        lax.all_gather(rows, TENSOR, axis=0, tiled=True),
+    )
+    received = lax.all_to_all(gathered, EXPERT, split_axis=1, concat_axis=1, tiled=True)
     return (received, rows_all)
 
 
 def from_experts(expert_part, shared_part):
-    returned = lax.all_to_all(expert_part, "expert", split_axis=1, concat_axis=1, tiled=True)
+    returned = lax.all_to_all(expert_part, EXPERT, split_axis=1, concat_axis=1, tiled=True)
     summed, shared_sum = (
-        lax.psum_scatter(returned, "tensor", scatter_dimension=0, tiled=True).astype(jnp.float32),
-        lax.psum_scatter(shared_part, "tensor", scatter_dimension=0, tiled=True).astype(
+        lax.psum_scatter(returned, TENSOR, scatter_dimension=0, tiled=True).astype(jnp.float32),
+        lax.psum_scatter(shared_part, TENSOR, scatter_dimension=0, tiled=True).astype(
             jnp.float32
         ),
     )
     return (summed, shared_sum)
 
 
-def per_device(
+def per_device_exchanged(
     inputs,
     norm_attn,
     w_query,
@@ -153,9 +158,9 @@
 ):
     own_rows = inputs.shape[0]
     width = inputs.shape[1]
-    tensor_size = lax.axis_size("tensor")
-    expert_size = lax.axis_size("expert")
-    tensor_index = lax.axis_index("tensor")
+    tensor_size = lax.axis_size(TENSOR)
+    expert_size = lax.axis_size(EXPERT)
+    tensor_index = lax.axis_index(TENSOR)
     seq_rows = own_rows * tensor_size
     local_heads = w_query.shape[1] // (NOPE + ROPE)
     experts = w_router.shape[1]
@@ -174,9 +179,9 @@
     cos_own, sin_own = rope_tables(tensor_index * own_rows + jnp.arange(own_rows), ROPE)
     rope_own = rotate(compressed[:, LATENT:], cos_own, sin_own).astype(jnp.bfloat16)
     h_all, lat_all, rope_all = (
-        lax.all_gather(h_own, "tensor", axis=0, tiled=True),
-        lax.all_gather(lat_own, "tensor", axis=0, tiled=True),
-        lax.all_gather(rope_own, "tensor", axis=0, tiled=True),
+        lax.all_gather(h_own, TENSOR, axis=0, tiled=True),
+        lax.all_gather(lat_own, TENSOR, axis=0, tiled=True),
+        lax.all_gather(rope_own, TENSOR, axis=0, tiled=True),
     )
     cos_all, sin_all = rope_tables(jnp.arange(seq_rows), ROPE)
     cos_all = cos_all[:, None, :]
@@ -203,7 +208,7 @@
         "sv,dv->sd", attended_flat, w_output, preferred_element_type=jnp.float32
     )
     after_attn = flat_in + lax.psum_scatter(
-        attn_terms.astype(jnp.bfloat16), "tensor", scatter_dimension=0, tiled=True
+        attn_terms.astype(jnp.bfloat16), TENSOR, scatter_dimension=0, tiled=True
     ).astype(jnp.float32)
     scale_two = lax.rsqrt(jnp.mean(after_attn * after_attn, axis=-1, keepdims=True) + EPS)
     normed_two = after_attn * scale_two
@@ -310,7 +315,7 @@
     grad_mid, grad_norm_moe = norm_back(grad_moe, normed_two, scale_two, norm_moe)
     grad_mid = grad_mid + grad_out
     grad_attn = grad_mid.astype(jnp.bfloat16)
-    grad_attn_all = lax.all_gather(grad_attn, "tensor", axis=0, tiled=True)
+    grad_attn_all = lax.all_gather(grad_attn, TENSOR, axis=0, tiled=True)
     grad_output = jnp.einsum(
         "sd,sv->dv", grad_attn_all, attended_flat, preferred_element_type=jnp.float32
     )
@@ -343,13 +348,13 @@
     )
     grad_h_own, grad_lat_own, grad_rope_own = (
         lax.psum_scatter(
-            grad_h_part.astype(jnp.bfloat16), "tensor", scatter_dimension=0, tiled=True
+            grad_h_part.astype(jnp.bfloat16), TENSOR, scatter_dimension=0, tiled=True
         ).astype(jnp.float32),
         lax.psum_scatter(
-            grad_lat_part.astype(jnp.bfloat16), "tensor", scatter_dimension=0, tiled=True
+            grad_lat_part.astype(jnp.bfloat16), TENSOR, scatter_dimension=0, tiled=True
         ).astype(jnp.float32),
         lax.psum_scatter(
-            grad_rope_part.astype(jnp.bfloat16), "tensor", scatter_dimension=0, tiled=True
+            grad_rope_part.astype(jnp.bfloat16), TENSOR, scatter_dimension=0, tiled=True
         ).astype(jnp.float32),
     )
     grad_lat_raw, grad_norm_latent = norm_back(grad_lat_own, normed_lat, scale_lat, norm_latent)
@@ -366,30 +371,30 @@
     grad_inputs = grad_mid + grad_in
     grad_query, grad_expand, grad_output, grad_shared_gate, grad_shared_up, grad_shared_down = (
         lax.psum_scatter(
-            grad_query.astype(jnp.bfloat16), "expert", scatter_dimension=0, tiled=True
+            grad_query.astype(jnp.bfloat16), EXPERT, scatter_dimension=0, tiled=True
         ).astype(jnp.float32),
         lax.psum_scatter(
-            grad_expand.astype(jnp.bfloat16), "expert", scatter_dimension=0, tiled=True
+            grad_expand.astype(jnp.bfloat16), EXPERT, scatter_dimension=0, tiled=True
         ).astype(jnp.float32),
         lax.psum_scatter(
-            grad_output.astype(jnp.bfloat16), "expert", scatter_dimension=0, tiled=True
+            grad_output.astype(jnp.bfloat16), EXPERT, scatter_dimension=0, tiled=True
         ).astype(jnp.float32),
         lax.psum_scatter(
-            grad_shared_gate.astype(jnp.bfloat16), "expert", scatter_dimension=0, tiled=True
+            grad_shared_gate.astype(jnp.bfloat16), EXPERT, scatter_dimension=0, tiled=True
         ).astype(jnp.float32),
         lax.psum_scatter(
-            grad_shared_up.astype(jnp.bfloat16), "expert", scatter_dimension=0, tiled=True
+            grad_shared_up.astype(jnp.bfloat16), EXPERT, scatter_dimension=0, tiled=True
         ).astype(jnp.float32),
         lax.psum_scatter(
-            grad_shared_down.astype(jnp.bfloat16), "expert", scatter_dimension=0, tiled=True
+            grad_shared_down.astype(jnp.bfloat16), EXPERT, scatter_dimension=0, tiled=True
         ).astype(jnp.float32),
     )
     grad_latent, grad_router, grad_norm_attn, grad_norm_moe, grad_norm_latent = (
-        lax.psum_scatter(grad_latent, ("expert", "tensor"), scatter_dimension=0, tiled=True),
-        lax.psum_scatter(grad_router, ("expert", "tensor"), scatter_dimension=0, tiled=True),
-        lax.psum_scatter(grad_norm_attn, ("expert", "tensor"), scatter_dimension=0, tiled=True),
-        lax.psum_scatter(grad_norm_moe, ("expert", "tensor"), scatter_dimension=0, tiled=True),
-        lax.psum_scatter(grad_norm_latent, ("expert", "tensor"), scatter_dimension=0, tiled=True),
+        lax.psum_scatter(grad_latent, (EXPERT, TENSOR), scatter_dimension=0, tiled=True),
+        lax.psum_scatter(grad_router, (EXPERT, TENSOR), scatter_dimension=0, tiled=True),
+        lax.psum_scatter(grad_norm_attn, (EXPERT, TENSOR), scatter_dimension=0, tiled=True),
+        lax.psum_scatter(grad_norm_moe, (EXPERT, TENSOR), scatter_dimension=0, tiled=True),
+        lax.psum_scatter(grad_norm_latent, (EXPERT, TENSOR), scatter_dimension=0, tiled=True),
     )
     return (
         output,
@@ -411,46 +416,1118 @@
     )
 
 
+PLANES = 4
+
+
+def send_core(values):
+    return lax.ppermute(values, TENSOR, [(0, 1), (1, 0)])
+
+
+def product(form, left, right):
+    return jnp.einsum(form, left, right, preferred_element_type=jnp.float32)
+
+
+EXTRA = 128
+VMEM_LIMIT = 54 << 20
+MESH = pl.DeviceIdType.MESH
+
+
+def dot(left, right):
+    return jnp.dot(left, right, preferred_element_type=jnp.float32)
+
+
+def dot_nt(left, right):
+    return lax.dot_general(
+        left, right, (((1,), (1,)), ((), ())), preferred_element_type=jnp.float32
+    )
+
+
+def dot_tn(left, right):
+    return lax.dot_general(
+        left, right, (((0,), (0,)), ((), ())), preferred_element_type=jnp.float32
+    )
+
+
+class Chips:
+    def __init__(self):
+        index = lax.axis_index(EXPERT)
+        self.z, self.y, self.x = index // 4, (index // 2) % 2, index % 2
+        self.core = lax.axis_index(TENSOR)
+        self.to_x = {EXPERT: self.at(self.z, self.y, 1 - self.x)}
+        self.to_y = {EXPERT: self.at(self.z, 1 - self.y, self.x)}
+        self.to_core = {TENSOR: 1 - self.core}
+
+    def at(self, z, y, x):
+        return (z * 2 + y) * 2 + x
+
+    def to_z(self, distance):
+        return {EXPERT: self.at((self.z + distance) % PLANES, self.y, self.x)}
+
+    def places(self, step):
+        plane = (self.z + PLANES - step) % PLANES
+        x, y = self.x, self.y
+        return [
+            self.at(plane, row, column)
+            for row, column in ((y, x), (y, 1 - x), (1 - y, x), (1 - y, 1 - x))
+        ]
+
+
+def greet(partners):
+    barrier = pltpu.get_barrier_semaphore()
+    for partner in partners:
+        pl.semaphore_signal(barrier, inc=1, device_id=partner, device_id_type=MESH)
+    pl.semaphore_wait(barrier, len(partners))
+
+
+def add_rows(target, terms):
+    @pl.loop(0, target.shape[0] // 16)
+    def _(chunk):
+        rows = pl.ds(pl.multiple_of(chunk * 16, 16), 16)
+        total = terms[0][rows, :].astype(jnp.float32)
+        for term in terms[1:]:
+            total = total + term[rows, :].astype(jnp.float32)
+        target[rows, :] = total.astype(target.dtype)
+
+
+def sum_kernel(parts, exchanged, *refs):
+    chips = Chips()
+    refs = list(refs)
+    arrays = 1 + max(part[0] for part in parts)
+    kind_of = {part[0]: part[1] for part in parts}
+    sources = [[refs.pop(0) for _ in range(2 if kind_of[a] == 2 else 1)] for a in range(arrays)]
+    blocks = refs.pop(0) if exchanged else None
+    results = [refs.pop(0) for _ in range(arrays)]
+    arrived = refs.pop(0) if exchanged else None
+    boxes = []
+    for _, kind, _, _, _ in parts:
+        mine = refs.pop(0)
+        from_core = refs.pop(0) if kind else None
+        boxes.append((mine, from_core) + tuple(refs.pop(0) for _ in range(4)))
+    if exchanged:
+        by_x, by_y, x_send, x_recv, z_send, z_recv = [refs.pop(0) for _ in range(6)]
+    load_sem, send_sem, recv_sem = refs
+    each = list(range(len(parts)))
+
+    def copy_to(source, target, send, recv, to):
+        return pltpu.make_async_remote_copy(
+            src_ref=source,
+            dst_ref=target,
+            send_sem=send,
+            recv_sem=recv,
+            device_id=to,
+            device_id_type=MESH,
+        )
+
+    def remote(part, step, index, source, target, to):
+        sems = (send_sem.at[part, step, index], recv_sem.at[part, step, index])
+        return copy_to(source, target, *sems, to)
+
+    def loads(part, step):
+        array, kind, start, stop, _ = parts[part]
+        mine, source = boxes[part][0], sources[array]
+        for k, place in enumerate(chips.places(step)):
+            if kind == 2:
+                block = source[0].at[step, k, :, start:stop]
+            elif kind == 1:
+                block = source[0].at[place, chips.core, :, start:stop]
+            else:
+                block = source[0].at[place, :, start:stop]
+            yield pltpu.make_async_copy(block, mine.at[step, k], load_sem.at[part, step, k])
+
+    def core_copies(part, step):
+        array, kind, start, stop, _ = parts[part]
+        if kind == 0:
+            return
+        for k, place in enumerate(chips.places(step)):
+            if kind == 2:
+                block = sources[array][1].at[step, k, :, start:stop]
+            else:
+                block = sources[array][0].at[place, 1 - chips.core, :, start:stop]
+            target = boxes[part][1].at[step, k]
+            yield remote(part, step, k, block, target, chips.to_core)
+
+    def level(part, step):
+        return 0 if parts[part][4] else step
+
+    def corner_copies(part, step):
+        mine, _, corners = boxes[part][:3]
+        half = mine.shape[2] // 2
+        here = corners.at[level(part, step)]
+        yield remote(part, step, 4, mine.at[step, 3, :half], here.at[0], chips.to_y)
+        yield remote(part, step, 5, mine.at[step, 3, half:], here.at[1], chips.to_x)
+
+    def early_copies(part, step):
+        mine, from_x, from_y = boxes[part][0], boxes[part][3], boxes[part][4]
+        half = mine.shape[2] // 2
+        x, y = from_x.at[level(part, step)], from_y.at[level(part, step)]
+        yield remote(part, step, 6, mine.at[step, 1, half:], x.at[half:], chips.to_x)
+        yield remote(part, step, 7, mine.at[step, 2, :half], y.at[:half], chips.to_y)
+
+    def late_copies(part, step):
+        mine, from_x, from_y = boxes[part][0], boxes[part][3], boxes[part][4]
+        half = mine.shape[2] // 2
+        x, y = from_x.at[level(part, step)], from_y.at[level(part, step)]
+        yield remote(part, step, 9, mine.at[step, 1, :half], x.at[:half], chips.to_x)
+        yield remote(part, step, 10, mine.at[step, 2, half:], y.at[half:], chips.to_y)
+
+    def side_copies(part, step):
+        return [*early_copies(part, step), *late_copies(part, step)]
+
+    def z_copy(part, step):
+        mine, from_z = boxes[part][0], boxes[part][5]
+        source = mine.at[step] if parts[part][4] else mine.at[step, 0]
+        return remote(part, step, 8, source, from_z.at[step - 1], chips.to_z(1))
+
+    def x_copy():
+        return copy_to(
+            blocks.at[:, :, 1 - chips.x], by_x, x_send.at[0], x_recv.at[0], chips.to_x
+        )
+
+    def y_copies():
+        own = blocks.at[:, 1 - chips.y, chips.x]
+        passed = by_x.at[:, 1 - chips.y]
+        return [
+            copy_to(source, by_y.at[k], x_send.at[1 + k], x_recv.at[1 + k], chips.to_y)
+            for k, source in enumerate((own, passed))
+        ]
+
+    def gathered(plane):
+        return [
+            blocks.at[plane, chips.y, chips.x],
+            by_x.at[plane, chips.y],
+            by_y.at[0, plane],
+            by_y.at[1, plane],
+        ]
+
+    def z_sends(distance):
+        plane = (chips.z + distance) % PLANES
+        return [
+            copy_to(
+                source,
+                arrived.at[place],
+                z_send.at[distance, k],
+                z_recv.at[distance, k],
+                chips.to_z(distance),
+            )
+            for k, (source, place) in enumerate(zip(gathered(plane), chips.places(0)))
+        ]
+
+    def z_arrivals(distance):
+        plane = (chips.z + distance) % PLANES
+        return [
+            copy_to(
+                source,
+                arrived.at[place],
+                z_send.at[distance, k],
+                z_recv.at[distance, k],
+                chips.to_z(distance),
+            )
+            for k, (source, place) in enumerate(zip(gathered(plane), chips.places(distance)))
+        ]
+
+    def keeps():
+        return [
+            pltpu.make_async_copy(source, arrived.at[place], z_send.at[0, k])
+            for k, (source, place) in enumerate(zip(gathered(chips.z), chips.places(0)))
+        ]
+
+    order = [*range(1, PLANES), 0]
+    distances = range(1, PLANES) if exchanged else (1, PLANES - 1)
+    greet([chips.to_x, chips.to_y, chips.to_core] + [chips.to_z(k) for k in distances])
+    if exchanged:
+        x_copy().start()
+
+    def fetch(step):
+        for part in each:
+            for copy in core_copies(part, step):
+                copy.start()
+            for copy in loads(part, step):
+                copy.start(priority=1)
+
+    fetch(order[0])
+    fetch(order[1])
+
+    def chip_sum(step):
+        ahead = order.index(step) + 2
+        for part in each:
+            mine, from_core = boxes[part][:2]
+            for copy in loads(part, step):
+                copy.wait()
+            for copy in core_copies(part, step):
+                copy.wait_recv()
+            for k in (3, 1, 2, 0):
+                if from_core is not None:
+                    add_rows(mine.at[step, k], [mine.at[step, k], from_core.at[step, k]])
+                if k == 3 and not parts[part][4]:
+                    for copy in corner_copies(part, step):
+                        copy.start()
+            if not parts[part][4]:
+                for copy in early_copies(part, step):
+                    copy.start()
+        if ahead < PLANES:
+            fetch(order[ahead])
+
+    def z_sum(step):
+        for part in each:
+            if parts[part][4]:
+                part_z_sum(part, step)
+
+    def part_z_sum(part, step):
+        mine, from_z = boxes[part][0], boxes[part][5]
+        if step != 1:
+            before = (step - 1) % PLANES
+            z_copy(part, before).wait_recv()
+            for k in (3, 1, 2, 0):
+                add_rows(mine.at[step, k], [mine.at[step, k], from_z.at[before - 1, k]])
+        if step:
+            z_copy(part, step).start()
+        else:
+            for copy in [*corner_copies(part, step), *early_copies(part, step)]:
+                copy.start()
+
+    def side_sum(step):
+        for part in each:
+            if parts[part][4] and step:
+                continue
+            mine, _, corners = boxes[part][:3]
+            half = mine.shape[2] // 2
+            for copy in corner_copies(part, step):
+                copy.wait_recv()
+            low_half, high_half = mine.at[step, 1, :half], mine.at[step, 2, half:]
+            here = corners.at[level(part, step)]
+            add_rows(low_half, [low_half, here.at[0]])
+            add_rows(high_half, [high_half, here.at[1]])
+            for copy in late_copies(part, step):
+                copy.start()
+
+    def plane_sum(step):
+        for part in each:
+            array, _, start, stop, along_z = parts[part]
+            if along_z and step:
+                continue
+            mine, _, _, from_x, from_y, from_z = boxes[part]
+            here = level(part, step)
+            terms = [mine.at[step, 0], from_x.at[here], from_y.at[here]]
+            for copy in side_copies(part, step):
+                copy.wait_recv()
+            if step != 1 and not along_z:
+                before = (step - 1) % PLANES
+                z_copy(part, before).wait_recv()
+                terms.append(from_z.at[before - 1])
+            if step == 0:
+                add_rows(results[array].at[:, start:stop], terms)
+            else:
+                add_rows(mine.at[step, 0], terms)
+                z_copy(part, step).start()
+
+    stages = ((0, chip_sum), (1, side_sum), (0, z_sum), (2, plane_sum))
+    for tick in range(PLANES + 2):
+        for late, stage in stages:
+            if 0 <= tick - late < PLANES:
+                stage(order[tick - late])
+        if exchanged and tick == 0:
+            x_copy().wait_recv()
+            for copy in y_copies():
+                copy.start()
+        if exchanged and tick == 1:
+            for copy in y_copies():
+                copy.wait_recv()
+            for copy in keeps():
+                copy.start()
+            for distance in range(1, PLANES):
+                for copy in z_sends(distance):
+                    copy.start()
+    if exchanged:
+        for copy in [x_copy(), *y_copies()]:
+            copy.wait_send()
+        for copy in keeps():
+            copy.wait()
+        for distance in range(1, PLANES):
+            for copy in z_arrivals(distance):
+                copy.wait_recv()
+            for copy in z_sends(distance):
+                copy.wait_send()
+    for part in each:
+        along_z = parts[part][4]
+        for step in range(PLANES):
+            sent = [*core_copies(part, step)]
+            if step == 0 or not along_z:
+                sent += [*corner_copies(part, step), *side_copies(part, step)]
+            if step:
+                sent.append(z_copy(part, step))
+            for copy in sent:
+                copy.wait_send()
+
+
+def sum_over_chips(collective_id, arrays, blocks=None):
+    low = jnp.bfloat16
+    parts, scratch, shapes = [], [], []
+    for index, (kind, operands, z_columns) in enumerate(arrays):
+        rows, columns = operands[0].shape[-2:]
+        shapes.append((rows, columns))
+        for start, stop in ((0, columns - z_columns), (columns - z_columns, columns)):
+            if start == stop:
+                continue
+            along_z = start > 0
+            parts.append((index, kind, start, stop, along_z))
+            size = (rows, stop - start)
+            levels = 1 if along_z else PLANES
+            scratch += [pltpu.VMEM((PLANES, 4) + size, low)] * (2 if kind else 1)
+            scratch += [
+                pltpu.VMEM((levels, 2, rows // 2, stop - start), low),
+                pltpu.VMEM((levels,) + size, low),
+                pltpu.VMEM((levels,) + size, low),
+                pltpu.VMEM((PLANES - 1,) + ((4,) if along_z else ()) + size, low),
+            ]
+    operands = [operand for _, group, _ in arrays for operand in group]
+    out_shape = [jax.ShapeDtypeStruct(shape, jnp.float32) for shape in shapes]
+    out_specs = [pl.BlockSpec(memory_space=pltpu.VMEM)] * len(shapes)
+    if blocks is not None:
+        operands.append(blocks)
+        block = blocks.shape[3:]
+        out_shape.append(jax.ShapeDtypeStruct((PLANES * 4,) + block, low))
+        out_specs.append(pl.BlockSpec(memory_space=pl.ANY))
+        scratch += [
+            pltpu.VMEM((PLANES, 2) + block, low),
+            pltpu.VMEM((2, PLANES) + block, low),
+            pltpu.SemaphoreType.DMA((3,)),
+            pltpu.SemaphoreType.DMA((3,)),
+            pltpu.SemaphoreType.DMA((PLANES, 4)),
+            pltpu.SemaphoreType.DMA((PLANES, 4)),
+        ]
+    size = sum(rows * columns for rows, columns in shapes)
+    semaphores = (len(parts), PLANES, 11)
+    return pl.pallas_call(
+        functools.partial(sum_kernel, tuple(parts), blocks is not None),
+        in_specs=[pl.BlockSpec(memory_space=pl.ANY)] * len(operands),
+        out_specs=out_specs,
+        out_shape=out_shape,
+        scratch_shapes=scratch
+        + [
+            pltpu.SemaphoreType.DMA((len(parts), PLANES, 4)),
+            pltpu.SemaphoreType.DMA(semaphores),
+            pltpu.SemaphoreType.DMA(semaphores),
+        ],
+        compiler_params=pltpu.CompilerParams(
+            collective_id=collective_id, has_side_effects=True, vmem_limit_bytes=VMEM_LIMIT
+        ),
+        cost_estimate=pl.CostEstimate(
+            flops=size * 30, bytes_accessed=size * 64, transcendentals=0
+        ),
+    )(*operands)
+
+
+def gated(gate_act, up_act, grad_hidden):
+    sigma = jax.nn.sigmoid(gate_act)
+    silu = gate_act * sigma
+    hidden = silu * up_act
+    grad_gate = grad_hidden * up_act * sigma * (1.0 + gate_act * (1.0 - sigma))
+    grad_up = grad_hidden * silu
+    return tuple(v.astype(jnp.bfloat16) for v in (hidden, grad_gate, grad_up))
+
+
+def moe_kernel(own_rows_in, lanes, w_gate, w_up, w_down, sw_gate, sw_up, sw_down, *refs):
+    land, out_mine, out_other, grad_mine, grad_other = refs[:5]
+    rows_out, pairs_out, hidden_out, gate_out, up_out, shared_out = refs[5:11]
+    rows_kept, grads_kept, out_kept, back_kept, extra_kept, s_hidden, s_grads, seats = refs[11:19]
+    x_here, g_here, gate_here, up_here, down_here, s_in, s_down, sum_in, sum_down = refs[19:28]
+    come, go, fetch, send_sem, recv_sem, z_send, z_recv = refs[28:]
+    width, half = s_down.shape
+    plane, step = pl.program_id(0), pl.program_id(1)
+    experts, slots = out_kept.shape[:2]
+    pairs, pair_rows_all, pair_slots = seats.shape
+    own = slots // pairs
+    low = jnp.bfloat16
+    chips = Chips()
+
+    def remote(step, index, source, target, to):
+        return pltpu.make_async_remote_copy(
+            src_ref=source,
+            dst_ref=target,
+            send_sem=send_sem.at[step, index],
+            recv_sem=recv_sem.at[step, index],
+            device_id=to,
+            device_id_type=MESH,
+        )
+
+    def own_block(step):
+        return own_rows_in if isinstance(step, int) and step == 0 else land.at[step, 0, 0]
+
+    def side_copies(step):
+        block = own_block(step)
+        return [
+            remote(step, 0, block, land.at[step, 0, 1], chips.to_x),
+            remote(step, 1, block, land.at[step, 0, 2], chips.to_y),
+        ]
+
+    def corner_copies(step):
+        return [
+            remote(step, 2, land.at[step, 0, 1, 0], land.at[step, 0, 3, 0], chips.to_y),
+            remote(step, 3, land.at[step, 0, 2, 1], land.at[step, 0, 3, 1], chips.to_x),
+        ]
+
+    def core_copy(step, k):
+        if k < 3:
+            source, target = land.at[step, 0, k] if k else own_block(step), land.at[step, 1, k]
+        else:
+            source, target = land.at[step, 0, 3, k - 3], land.at[step, 1, 3, k - 3]
+        return remote(step, 4 + k, source, target, chips.to_core)
+
+    def z_copy(k):
+        return pltpu.make_async_remote_copy(
+            src_ref=own_block(k - 1),
+            dst_ref=land.at[k, 0, 0],
+            send_sem=z_send.at[k],
+            recv_sem=z_recv.at[k],
+            device_id=chips.to_z(1),
+            device_id_type=MESH,
+        )
+
+    def start_plane(step):
+        for copy in side_copies(step) + [core_copy(step, 0)]:
+            copy.start()
+
+    def pass_corners(step):
+        for copy in side_copies(step):
+            copy.wait_recv()
+        for copy in corner_copies(step) + [core_copy(step, 1), core_copy(step, 2)]:
+            copy.start()
+
+    def finish_plane(step):
+        for copy in corner_copies(step):
+            copy.wait_recv()
+        for k in (3, 4):
+            core_copy(step, k).start()
+        for k in range(5):
+            core_copy(step, k).wait_recv()
+
+    def weight_copies(expert):
+        return [
+            pltpu.make_async_copy(source.at[expert], target.at[expert], fetch.at[expert, k])
+            for k, (source, target) in enumerate(
+                ((w_gate, gate_here), (w_up, up_here), (w_down, down_here))
+            )
+        ]
+
+    shared_blocks = sw_gate.shape[1] // half
+    chip = chips.at(chips.z, chips.y, chips.x)
+    shared_here = chip < shared_blocks
+
+    def shared_copies():
+        columns = pl.ds(pl.multiple_of((chip % shared_blocks) * half, half), half)
+        return [
+            pltpu.make_async_copy(source.at[:, columns], target, fetch.at[experts, k])
+            for k, (source, target) in enumerate(
+                (
+                    (sw_gate, s_in.at[:, :half]),
+                    (sw_up, s_in.at[:, half:]),
+                    (sw_down, s_down),
+                )
+            )
+        ]
+
+    @pl.when((plane == 0) & (step == 0))
+    def _():
+        greet(
+            [chips.to_x, chips.to_y, chips.to_core, chips.to_z(1), chips.to_z(PLANES - 1)]
+        )
+        start_plane(0)
+        z_copy(1).start()
+
+        @pl.when(shared_here)
+        def _():
+            for copy in shared_copies():
+                copy.start()
+
+        for expert in range(experts):
+            for copy in weight_copies(expert):
+                copy.start()
+        pass_corners(0)
+        z_copy(1).wait_recv()
+        z_copy(2).start()
+        start_plane(1)
+
+        @pl.when(shared_here)
+        def _():
+            for copy in shared_copies():
+                copy.wait()
+
+        @pl.when(~shared_here)
+        def _():
+            s_in[...] = jnp.zeros(s_in.shape, low)
+            s_down[...] = jnp.zeros(s_down.shape, low)
+
+        finish_plane(0)
+
+    def pair_place(pair):
+        return pair // (pairs // 2), slice((pair % (pairs // 2)) * 2, (pair % (pairs // 2)) * 2 + 2)
+
+    def coming(pair):
+        side, blocks = pair_place(pair)
+        return [
+            pltpu.make_async_copy(
+                land.at[plane, side, blocks, which],
+                here.at[2 * pair : 2 * pair + 2],
+                come.at[which * pairs + pair],
+            )
+            for which, here in enumerate((x_here, g_here))
+        ]
+
+    def going(pair):
+        side, blocks = pair_place(pair)
+        return [
+            pltpu.make_async_copy(
+                here.at[2 * pair : 2 * pair + 2, :, :columns],
+                targets[side].at[plane, blocks],
+                go.at[which * pairs + pair],
+            )
+            for which, (targets, here, columns) in enumerate(
+                (
+                    ((out_mine, out_other), x_here, width),
+                    ((grad_mine, grad_other), g_here, width + EXTRA),
+                )
+            )
+        ]
+
+    def pair_rows(here, pair, columns):
+        return here[2 * pair : 2 * pair + 2, :, :columns].reshape(pair_rows_all, columns)
+
+    def own_coming():
+        for which, here in enumerate((x_here, g_here)):
+            for block, source in enumerate((own_rows_in.at[which], land.at[0, 0, 1, which])):
+                yield pltpu.make_async_copy(source, here.at[block], come.at[which * pairs])
+
+    @pl.when((step == 0) & (plane == 0))
+    def _():
+        for copy in own_coming():
+            copy.start()
+
+    @pl.when((step == 0) & (plane > 0))
+    def _():
+        for copy in coming(0):
+            copy.start()
+
+    @pl.when(step == 0)
+    def _():
+        for pair in range(1, pairs):
+            for copy in coming(pair):
+                copy.start()
+        tokens = lax.broadcasted_iota(jnp.int32, (pair_rows_all, pair_rows_all), 0)
+        others = lax.broadcasted_iota(jnp.int32, (pair_rows_all, pair_rows_all), 1)
+        own_rows = pair_rows_all // 2
+        earlier = (others < tokens) & ((others >= own_rows) == (tokens >= own_rows))
+        earlier = earlier.astype(jnp.float32).astype(low)
+        lane = lax.broadcasted_iota(jnp.int32, (pair_rows_all, pair_slots), 1)
+        block = lax.broadcasted_iota(jnp.int32, (pair_rows_all, pair_slots), 0) // own_rows
+        capacity = own // 2
+        at_block = lax.rem(lane // capacity, 2) == block
+        at_slot = lax.rem(lane, capacity).astype(jnp.float32)
+        for pair in range(pairs):
+            for copy in coming(pair):
+                copy.wait()
+            grads = pair_rows(g_here, pair, width + EXTRA)
+            routes = grads[:, width:].astype(jnp.float32)
+            named = routes[:, :1] == lanes[:1]
+            for k in range(1, TOPK):
+                named = named | (routes[:, k : k + 1] == lanes[:1])
+            named = named.astype(jnp.float32)
+            rank = dot(earlier, named.astype(low))
+            seat = jnp.where(at_block & (rank == at_slot), named, 0.0).astype(low)
+            seats[pair] = seat
+            rows = dot_tn(seat, pair_rows(x_here, pair, width + EXTRA))
+            grads = dot_tn(seat, grads[:, :width])
+            for expert in range(experts):
+                here = slice(expert * own, (expert + 1) * own)
+                there = slice(pair * own, (pair + 1) * own)
+                low_rows = rows[here, :width].astype(jnp.bfloat16)
+                low_grads = grads[here].astype(jnp.bfloat16)
+                if expert == 0:
+                    rows_out[0, there] = low_rows
+                    pairs_out[0, there] = low_grads
+                else:
+                    rows_kept[expert - 1, there] = low_rows
+                    grads_kept[expert - 1, there] = low_grads
+                gate = jnp.sum(
+                    rows[here, width:] * lanes[1 + expert : 2 + expert], axis=-1, keepdims=True
+                )
+                extra_kept[expert, there] = jnp.broadcast_to(gate, (own, EXTRA))
+        for side in range(2):
+            blocks = slice(side * pairs, (side + 1) * pairs)
+            tokens = pairs * own_rows
+            rows = x_here[blocks, :, :width].reshape(tokens, width)
+            grads = g_here[blocks, :, :width].reshape(tokens, width)
+            acts = dot(rows, s_in[...])
+            hidden, grad_gate, grad_up = gated(
+                acts[:, :half], acts[:, half:], dot(grads, s_down[...])
+            )
+            s_hidden[side * tokens : (side + 1) * tokens] = hidden
+            both = jnp.concatenate([grad_gate, grad_up], axis=1)
+            s_grads[side * tokens : (side + 1) * tokens] = both
+            term_in, term_down = dot_tn(both, rows), dot_tn(hidden, grads)
+            if side == 0:
+                fresh = plane == 0
+                sum_in[...] = jnp.where(fresh, 0.0, sum_in[...]) + term_in
+                sum_down[...] = jnp.where(fresh, 0.0, sum_down[...]) + term_down
+            else:
+                sum_in[...] += term_in
+                sum_down[...] += term_down
+
+    @pl.when(step > 0)
+    def _():
+        rows_out[0] = rows_kept[step - 1]
+        pairs_out[0] = grads_kept[step - 1]
+
+    @pl.when(plane == 0)
+    def _():
+        for copy in weight_copies(step):
+            copy.wait()
+
+    rows = rows_out[0]
+    grads = pairs_out[0].astype(jnp.float32)
+    gates = extra_kept[step][:, :1]
+    pair_grads = (grads * gates).astype(jnp.bfloat16)
+    hidden, grad_gate, grad_up = gated(
+        dot_nt(rows, gate_here[step]), dot_nt(rows, up_here[step]), dot_nt(pair_grads, down_here[step])
+    )
+    hidden_out[0] = hidden
+    gate_out[0] = grad_gate
+    up_out[0] = grad_up
+    part = dot(hidden, down_here[step])
+    out_kept[step] = (part * gates).astype(jnp.bfloat16)
+    slot_grad = jnp.sum(part * grads, axis=-1, keepdims=True)
+    pairs_out[0] = pair_grads
+    high = slot_grad.astype(jnp.bfloat16).astype(jnp.float32)
+    lane_row = 1 + experts + step * 2
+    extra_kept[step] = high * lanes[pl.ds(lane_row, 1)] + (slot_grad - high) * lanes[
+        pl.ds(lane_row + 1, 1)
+    ]
+    back_kept[step] = (dot(grad_gate, gate_here[step]) + dot(grad_up, up_here[step])).astype(
+        jnp.bfloat16
+    )
+
+    @pl.when((step == 0) & (plane + 1 < PLANES))
+    def _():
+        pass_corners(plane + 1)
+
+    @pl.when((step == 0) & (plane + 2 < PLANES))
+    def _():
+        for k in range(2, PLANES):
+
+            @pl.when(plane == k - 2)
+            def _(k=k):
+                z_copy(k).wait_recv()
+                if k + 1 < PLANES:
+                    z_copy(k + 1).start()
+
+        start_plane(plane + 2)
+
+    @pl.when(step == experts - 1)
+    def _():
+        for pair in range(pairs):
+            there = slice(pair * own, (pair + 1) * own)
+            tokens = slice(pair * pair_rows_all, (pair + 1) * pair_rows_all)
+            here = slice(2 * pair, 2 * pair + 2)
+            back = seats[pair]
+            total = dot(
+                back, jnp.concatenate([out_kept[e, there] for e in range(experts)], 0)
+            ) + dot_nt(s_hidden[tokens], s_down[...])
+            x_here[here, :, :width] = total.astype(jnp.bfloat16).reshape(2, -1, width)
+            total = dot(
+                back, jnp.concatenate([back_kept[e, there] for e in range(experts)], 0)
+            ) + dot_nt(s_grads[tokens], s_in[...])
+            g_here[here, :, :width] = total.astype(jnp.bfloat16).reshape(
+                2, -1, width
+            )
+            extra = jnp.concatenate([extra_kept[e, there] for e in range(experts)], 0)
+            total = dot(back, extra.astype(jnp.bfloat16))
+            g_here[here, :, width:] = total.astype(jnp.bfloat16).reshape(2, -1, EXTRA)
+            for copy in going(pair):
+                copy.start()
+        for pair in range(pairs):
+            for copy in going(pair):
+                copy.wait()
+
+    @pl.when((step == experts - 1) & (plane + 1 < PLANES))
+    def _():
+        finish_plane(plane + 1)
+
+    @pl.when((step == experts - 1) & (plane == PLANES - 1))
+    def _():
+        block_rows = width // shared_out.shape[0]
+        for to in range(shared_out.shape[0]):
+            there = slice(to * block_rows, (to + 1) * block_rows)
+            shared_out[to, : 2 * half] = sum_in[:, there].astype(low)
+            shared_out[to, 2 * half :] = sum_down[:, there].astype(low)
+        for k in range(1, PLANES):
+            z_copy(k).wait_send()
+
+        @pl.loop(0, PLANES)
+        def _(sent):
+            for copy in side_copies(sent) + corner_copies(sent):
+                copy.wait_send()
+            for k in range(5):
+                core_copy(sent, k).wait_send()
+
+
+def moe_layer(own_rows_in, lanes, weights):
+    experts, units, width = weights[0].shape
+    _, own_rows, wide = own_rows_in.shape
+    blocks, pairs, pair_rows, pair_slots = 4, 4, 2 * own_rows, EXTRA
+    slots = pairs * pair_slots // experts
+    tokens = pairs * pair_rows
+    half = EXTRA
+    chips = lax.axis_size(EXPERT)
+    low = jnp.bfloat16
+
+    def whole(array):
+        zeros = (0,) * len(array.shape)
+        return pl.BlockSpec(array.shape, lambda s, j: zeros, pipeline_mode=pl.Buffered(1))
+
+    anywhere = pl.BlockSpec(memory_space=pl.ANY)
+    land = [jax.ShapeDtypeStruct((PLANES, 2, blocks, 2, own_rows, wide), low)]
+    plain = [jax.ShapeDtypeStruct((PLANES, blocks, own_rows, width), low)] * 2
+    extended = [jax.ShapeDtypeStruct((PLANES, blocks, own_rows, wide), low)] * 2
+    keep = [
+        jax.ShapeDtypeStruct((experts, PLANES * slots, columns), low)
+        for columns in (width, width, units, units, units)
+    ]
+    shared = [jax.ShapeDtypeStruct((chips, 3 * half, width // chips), low)]
+    operands = [own_rows_in, lanes] + list(weights)
+    work = 2 * tokens * width * (8 * half + 2 * pair_slots) + 12 * experts * slots * width * units
+    results = pl.pallas_call(
+        moe_kernel,
+        grid=(PLANES, experts),
+        in_specs=[anywhere, whole(lanes)] + [anywhere] * len(weights),
+        out_specs=[anywhere] * 5
+        + [pl.BlockSpec((1, slots, v.shape[2]), lambda s, j: (j, s, 0)) for v in keep]
+        + [whole(v) for v in shared],
+        out_shape=land + plain + extended + keep + shared,
+        scratch_shapes=[
+            pltpu.VMEM((experts - 1, slots, width), low),
+            pltpu.VMEM((experts - 1, slots, width), low),
+            pltpu.VMEM((experts, slots, width), low),
+            pltpu.VMEM((experts, slots, width), low),
+            pltpu.VMEM((experts, slots, EXTRA), jnp.float32),
+            pltpu.VMEM((tokens, half), low),
+            pltpu.VMEM((tokens, 2 * half), low),
+            pltpu.VMEM((pairs, pair_rows, pair_slots), low),
+            pltpu.VMEM((2 * blocks, own_rows, wide), low),
+            pltpu.VMEM((2 * blocks, own_rows, wide), low),
+            pltpu.VMEM(weights[0].shape, low),
+            pltpu.VMEM(weights[1].shape, low),
+            pltpu.VMEM(weights[2].shape, low),
+            pltpu.VMEM((width, 2 * half), low),
+            pltpu.VMEM((width, half), low),
+            pltpu.VMEM((2 * half, width), jnp.float32),
+            pltpu.VMEM((half, width), jnp.float32),
+            pltpu.SemaphoreType.DMA((2 * pairs,)),
+            pltpu.SemaphoreType.DMA((2 * pairs,)),
+            pltpu.SemaphoreType.DMA((experts + 1, 3)),
+            pltpu.SemaphoreType.DMA((PLANES, 9)),
+            pltpu.SemaphoreType.DMA((PLANES, 9)),
+            pltpu.SemaphoreType.DMA((PLANES,)),
+            pltpu.SemaphoreType.DMA((PLANES,)),
+        ],
+        compiler_params=pltpu.CompilerParams(
+            collective_id=0, has_side_effects=True, vmem_limit_bytes=VMEM_LIMIT
+        ),
+        cost_estimate=pl.CostEstimate(
+            flops=PLANES * work, bytes_accessed=120 << 20, transcendentals=0
+        ),
+    )(*operands)
+    return results[1:3], results[3:5], results[5:]
+
+
+def per_device_gathered(
+    inputs,
+    norm_attn,
+    w_query,
+    w_latent,
+    norm_latent,
+    w_expand,
+    w_output,
+    norm_moe,
+    w_router,
+    w_shared_gate,
+    w_shared_up,
+    w_shared_down,
+    w_expert_gate,
+    w_expert_up,
+    w_expert_down,
+    routes,
+    cotangent,
+):
+    own_rows = inputs.shape[0]
+    width = inputs.shape[1]
+    tensor_size = lax.axis_size(TENSOR)
+    expert_size = lax.axis_size(EXPERT)
+    tensor_index = lax.axis_index(TENSOR)
+    expert_index = lax.axis_index(EXPERT)
+    seq_rows = own_rows * tensor_size
+    local_heads = w_query.shape[1] // (NOPE + ROPE)
+    experts = w_router.shape[1]
+    local_experts = experts // expert_size
+    capacity = own_rows * TOPK * 4 // (3 * experts)
+    scale = 1.0 / math.sqrt(NOPE + ROPE)
+
+    flat_in = inputs.astype(jnp.float32)
+    scale_one = lax.rsqrt(jnp.mean(flat_in * flat_in, axis=-1, keepdims=True) + EPS)
+    normed_one = flat_in * scale_one
+    h_own = (normed_one * norm_attn).astype(jnp.bfloat16)
+    compressed = jnp.dot(h_own, w_latent, preferred_element_type=jnp.float32)
+    lat_raw = compressed[:, :LATENT]
+    scale_lat = lax.rsqrt(jnp.mean(lat_raw * lat_raw, axis=-1, keepdims=True) + EPS)
+    normed_lat = lat_raw * scale_lat
+    lat_own = (normed_lat * norm_latent).astype(jnp.bfloat16)
+    places = jnp.arange(own_rows)
+    places_all = jnp.concatenate(
+        [tensor_index * own_rows + places, (1 - tensor_index) * own_rows + places]
+    )
+    cos_own, sin_own = rope_tables(places_all[:own_rows], ROPE)
+    rope_own = rotate(compressed[:, LATENT:], cos_own, sin_own).astype(jnp.bfloat16)
+
+    def both(values):
+        return jnp.concatenate([values, send_core(values)], axis=0)
+
+    h_all = both(h_own)
+    lat_rope = both(jnp.concatenate([lat_own, rope_own], axis=1))
+    lat_all, rope_all = lat_rope[:, :LATENT], lat_rope[:, LATENT:]
+    cos_all, sin_all = rope_tables(places_all, ROPE)
+    cos_all = cos_all[:, None, :]
+    sin_all = sin_all[:, None, :]
+    query_raw = jnp.dot(h_all, w_query, preferred_element_type=jnp.float32).reshape(
+        seq_rows, local_heads, NOPE + ROPE
+    )
+    query = jnp.concatenate(
+        [query_raw[..., :NOPE], rotate(query_raw[..., NOPE:], cos_all, sin_all)], axis=-1
+    ).astype(jnp.bfloat16)
+    expanded = jnp.dot(lat_all, w_expand, preferred_element_type=jnp.float32).astype(jnp.bfloat16)
+    expanded = expanded.reshape(seq_rows, local_heads, NOPE + VD)
+    key_full = jnp.concatenate(
+        [
+            expanded[..., :NOPE],
+            jnp.broadcast_to(rope_all[:, None, :], (seq_rows, local_heads, ROPE)),
+        ],
+        axis=-1,
+    )
+    value = expanded[..., NOPE:]
+    allowed = (places_all[:, None] >= places_all[None, :])[None]
+    scores = product("qhd,khd->hqk", query, key_full) * scale
+    scores = jnp.where(allowed, scores, -1e30)
+    weights = jnp.exp(scores - jnp.max(scores, axis=-1, keepdims=True))
+    probs = weights / jnp.sum(weights, axis=-1, keepdims=True)
+    attended = product("hqk,khd->qhd", probs.astype(jnp.bfloat16), value)
+    attended_flat = attended.astype(jnp.bfloat16).reshape(seq_rows, local_heads * VD)
+    attn_terms = product("sv,dv->sd", attended_flat, w_output)
+    after_attn = (
+        flat_in
+        + attn_terms[:own_rows]
+        + send_core(attn_terms[own_rows:].astype(jnp.bfloat16)).astype(jnp.float32)
+    )
+    scale_two = lax.rsqrt(jnp.mean(after_attn * after_attn, axis=-1, keepdims=True) + EPS)
+    normed_two = after_attn * scale_two
+    h_moe = (normed_two * norm_moe).astype(jnp.bfloat16)
+    logits = jnp.dot(h_moe, w_router, preferred_element_type=jnp.float32)
+    expert_ids = jnp.arange(experts, dtype=jnp.int32)
+    chosen = jnp.any(routes[:, :, None] == expert_ids[None, None, :], axis=1)
+    masked = jnp.where(chosen, logits, -1e30)
+    raised = jnp.where(chosen, jnp.exp(masked - jnp.max(masked, axis=-1, keepdims=True)), 0.0)
+    gates = raised / jnp.sum(raised, axis=-1, keepdims=True)
+    high_gates = lax.reduce_precision(gates, 8, 7)
+    beside = jnp.stack(
+        [
+            jnp.pad(
+                jnp.concatenate([high_gates, gates - high_gates], axis=1),
+                ((0, 0), (0, EXTRA - 2 * experts)),
+            ),
+            jnp.pad(routes.astype(jnp.float32), ((0, 0), (0, EXTRA - TOPK))),
+        ]
+    ).astype(jnp.bfloat16)
+    own_rows_in = jnp.concatenate([jnp.stack([h_moe, cotangent]), beside], axis=2)
+
+    own_ids = expert_index * local_experts + jnp.arange(local_experts, dtype=jnp.int32)
+    lane_ids = jnp.arange(EXTRA, dtype=jnp.int32)[None, :]
+    slot_experts = expert_index * local_experts + lane_ids // (2 * capacity)
+    gate_lanes = (lane_ids == own_ids[:, None]) | (lane_ids == own_ids[:, None] + experts)
+    back_lanes = (own_ids[:, None] * tensor_size + tensor_index) * 2 + jnp.arange(2)[None, :]
+    lanes = jnp.concatenate(
+        [slot_experts, gate_lanes, lane_ids == back_lanes.reshape(-1, 1)], axis=0
+    ).astype(jnp.float32)
+    lanes = jnp.pad(lanes, ((0, -lanes.shape[0] % 8), (0, 0)))
+
+    all_weights = tuple(jnp.swapaxes(w, 1, 2) for w in (w_expert_gate, w_expert_up, w_expert_down))
+    all_weights += (w_shared_gate, w_shared_up, w_shared_down)
+    out_parts, grad_parts, kept = moe_layer(own_rows_in, lanes, all_weights)
+    shared_grads = kept[5].reshape((PLANES, 2, 2) + kept[5].shape[1:])
+    moe_back, moe_out, shared_grads = sum_over_chips(
+        1, [(2, grad_parts, 512), (2, out_parts, 512)], shared_grads
+    )
+    output = (after_attn + moe_out).astype(jnp.bfloat16)
+
+    grad_gates = jnp.sum(moe_back[:, width:].reshape(own_rows, experts, -1), axis=-1)
+    grad_gates = jnp.where(chosen, grad_gates, 0.0)
+    grad_select = gates * (grad_gates - jnp.sum(gates * grad_gates, axis=-1, keepdims=True))
+    grad_logits = grad_select.astype(jnp.bfloat16)
+    grad_router = product("td,te->de", h_moe, grad_logits)
+
+    grad_out = cotangent.astype(jnp.float32)
+    grad_moe = moe_back[:, :width] + product("te,de->td", grad_logits, w_router)
+    grad_mid, grad_norm_moe = norm_back(grad_moe, normed_two, scale_two, norm_moe)
+    grad_mid = grad_mid + grad_out
+    grad_attn_all = both(grad_mid.astype(jnp.bfloat16))
+    grad_output = product("sd,sv->dv", grad_attn_all, attended_flat)
+    grad_attended = product("sd,dv->sv", grad_attn_all, w_output)
+    grad_attended = grad_attended.astype(jnp.bfloat16).reshape(seq_rows, local_heads, VD)
+    grad_probs = product("qhv,khv->hqk", grad_attended, value)
+    centre = jnp.sum(probs * grad_probs, axis=-1, keepdims=True)
+    grad_scores = (probs * (grad_probs - centre)).astype(jnp.bfloat16)
+    grad_query_full = product("hqk,khd->qhd", grad_scores, key_full) * scale
+    grad_key_full = product("hqk,qhd->khd", grad_scores, query) * scale
+    grad_value = product("hqk,qhv->khv", probs.astype(jnp.bfloat16), grad_attended)
+    grad_query_raw = jnp.concatenate(
+        [grad_query_full[..., :NOPE], unrotate(grad_query_full[..., NOPE:], cos_all, sin_all)],
+        axis=-1,
+    )
+    grad_query_raw = grad_query_raw.astype(jnp.bfloat16).reshape(
+        seq_rows, local_heads * (NOPE + ROPE)
+    )
+    grad_query = product("sd,sq->dq", h_all, grad_query_raw)
+    grad_expanded = jnp.concatenate([grad_key_full[..., :NOPE], grad_value], axis=-1)
+    grad_expanded = grad_expanded.astype(jnp.bfloat16).reshape(seq_rows, local_heads * (NOPE + VD))
+    grad_expand = product("sl,sk->lk", lat_all, grad_expanded)
+    grad_rope_part = jnp.sum(grad_key_full[..., NOPE:], axis=1)
+    grad_h_part = product("sq,dq->sd", grad_query_raw, w_query)
+    grad_lat_part = product("sk,lk->sl", grad_expanded, w_expand)
+    own_side = jnp.concatenate([grad_lat_part, grad_rope_part], axis=1)
+    own_side = own_side[:own_rows] + send_core(own_side[own_rows:].astype(jnp.bfloat16)).astype(
+        jnp.float32
+    )
+    grad_h_own = grad_h_part[:own_rows] + send_core(
+        grad_h_part[own_rows:].astype(jnp.bfloat16)
+    ).astype(jnp.float32)
+    grad_lat_raw, grad_norm_latent = norm_back(
+        own_side[:, :LATENT], normed_lat, scale_lat, norm_latent
+    )
+    grad_compressed = jnp.concatenate(
+        [grad_lat_raw, unrotate(own_side[:, LATENT:], cos_own, sin_own)], axis=-1
+    ).astype(jnp.bfloat16)
+    grad_latent = product("td,tc->dc", h_own, grad_compressed)
+    grad_h = grad_h_own + product("tc,dc->td", grad_compressed, w_latent)
+    grad_in, grad_norm_attn = norm_back(grad_h, normed_one, scale_one, norm_attn)
+    grad_inputs = grad_mid + grad_in
+
+    share = width // expert_size
+    low_rows = expert_size * share
+    own_part = share // tensor_size
+
+    def in_two(values):
+        high = lax.reduce_precision(values, 8, 7)
+        return jnp.stack([high, values - high], axis=-1)
+
+    gains = in_two(grad_norm_latent).reshape(expert_size * tensor_size, -1, 2)
+    gain_rows = gains.shape[1]
+    gains = jnp.pad(gains, ((0, 0), (0, own_part - gain_rows), (0, 0))).reshape(low_rows, 2)
+    small = jnp.concatenate(
+        [grad_router, in_two(grad_norm_attn), in_two(grad_norm_moe), gains], axis=1
+    )
+    small = jnp.pad(small, ((0, 0), (0, EXTRA - small.shape[1])))
+    small, grad_latent = [
+        v.astype(jnp.bfloat16).reshape(expert_size, tensor_size, own_part, -1)
+        for v in (small, grad_latent)
+    ]
+    grad_output = grad_output.astype(jnp.bfloat16).reshape(expert_size, share, -1)
+    grad_query = grad_query.astype(jnp.bfloat16).reshape(expert_size, share, -1)
+    grad_expand = grad_expand.astype(jnp.bfloat16).reshape(expert_size, -1, w_expand.shape[1])
+    grad_output, grad_query, grad_expand, grad_latent, small = sum_over_chips(
+        2,
+        [
+            (0, [grad_output], 256),
+            (0, [grad_query], 384),
+            (0, [grad_expand], 512),
+            (1, [grad_latent], 0),
+            (1, [small], 0),
+        ],
+    )
+    grad_router = small[:, :experts]
+    grad_norm_attn = small[:, experts] + small[:, experts + 1]
+    grad_norm_moe = small[:, experts + 2] + small[:, experts + 3]
+    grad_norm_latent = (small[:, experts + 4] + small[:, experts + 5])[:gain_rows]
+
+    rows, pair_grads, hidden, grad_gate, grad_up = kept[:5]
+    grad_expert_down = product("jsd,jsf->jdf", pair_grads, hidden)
+    grad_expert_gate = product("jsd,jsf->jdf", rows, grad_gate)
+    grad_expert_up = product("jsd,jsf->jdf", rows, grad_up)
+    columns = w_shared_gate.shape[1]
+    shared_grads = shared_grads[: columns // EXTRA].reshape(-1, 3, EXTRA, share)
+    shared_grads = (
+        jnp.transpose(shared_grads, (1, 3, 0, 2)).reshape(3, share, columns).astype(jnp.float32)
+    )
+    return (
+        output,
+        grad_inputs,
+        grad_norm_attn,
+        grad_query,
+        grad_latent,
+        grad_norm_latent,
+        grad_expand,
+        grad_output,
+        grad_norm_moe,
+        grad_router,
+        shared_grads[0],
+        shared_grads[1],
+        shared_grads[2],
+        grad_expert_gate,
+        grad_expert_up,
+        grad_expert_down,
+    )
+
+
+def per_device_for(mesh):
+    if mesh.shape[EXPERT] == PLANES * 4 and mesh.shape[TENSOR] == 2:
+        return per_device_gathered
+    return per_device_exchanged
+
+
 def solution(mesh):
     return jax.shard_map(
-        per_device,
+        per_device_for(mesh),
         mesh=mesh,
         in_specs=(
-            P(("expert", "tensor"), None),
+            P((EXPERT, TENSOR), None),
             P(),
-            P(None, "tensor"),
+            P(None, TENSOR),
             P(),
             P(),
-            P(None, "tensor"),
-            P(None, "tensor"),
+            P(None, TENSOR),
+            P(None, TENSOR),
             P(),
             P(),
-            P(None, "tensor"),
-            P(None, "tensor"),
-            P(None, "tensor"),
-            P("expert", None, "tensor"),
-            P("expert", None, "tensor"),
-            P("expert", None, "tensor"),
-            P(("expert", "tensor"), None),
-            P(("expert", "tensor"), None),
+            P(None, TENSOR),
+            P(None, TENSOR),
+            P(None, TENSOR),
+            P(EXPERT, None, TENSOR),
+            P(EXPERT, None, TENSOR),
+            P(EXPERT, None, TENSOR),
+            P((EXPERT, TENSOR), None),
+            P((EXPERT, TENSOR), None),
         ),
         out_specs=(
-            P(("expert", "tensor"), None),
-            P(("expert", "tensor"), None),
-            P(("expert", "tensor")),
-            P("expert", "tensor"),
-            P(("expert", "tensor"), None),
-            P(("expert", "tensor")),
-            P("expert", "tensor"),
-            P("expert", "tensor"),
-            P(("expert", "tensor")),
-            P(("expert", "tensor"), None),
-            P("expert", "tensor"),
-            P("expert", "tensor"),
-            P("expert", "tensor"),
-            P("expert", None, "tensor"),
-            P("expert", None, "tensor"),
-            P("expert", None, "tensor"),
+            P((EXPERT, TENSOR), None),
+            P((EXPERT, TENSOR), None),
+            P((EXPERT, TENSOR)),
+            P(EXPERT, TENSOR),
+            P((EXPERT, TENSOR), None),
+            P((EXPERT, TENSOR)),
+            P(EXPERT, TENSOR),
+            P(EXPERT, TENSOR),
+            P((EXPERT, TENSOR)),
+            P((EXPERT, TENSOR), None),
+            P(EXPERT, TENSOR),
+            P(EXPERT, TENSOR),
+            P(EXPERT, TENSOR),
+            P(EXPERT, None, TENSOR),
+            P(EXPERT, None, TENSOR),
+            P(EXPERT, None, TENSOR),
         ),
         check_vma=False,
     )

time: 2240 us -> 651 us (0.29)
  waiting for transfers between devices: 1290 us -> 0.84 us
  Pallas kernels: 0 us -> 483 us
  blocking collectives: 267 us -> 0 us
  local copies, waits for them, and re-layouts: 272 us -> 50.2 us
  matrix products: 238 us -> 82.6 us
  starting transfers between devices: 87.5 us -> 2.16 us
  other arithmetic: 66.3 us -> 21.8 us
    reduce_scatter x10 -> x0, waiting for transfers between devices: 697 us -> none  [the longest x1 149 us: per_device(): lax.psum_scatter(grad_query.astype(jnp.bfloat16), 'expert', scatter_dimen...]
    pallas_call x0 -> x3, Pallas kernels: none -> 483 us  [the longest x2 287 us: sum_over_chips(): pl.pallas_call(functools.partial(sum_kernel, tuple(parts), blocks is not...]
    all_to_all x3 -> x0, waiting for transfers between devices: 359 us -> none  [the longest x2 209 us: to_experts(): lax.all_to_all(gathered, 'expert', split_axis=1, concat_axis=1, tiled=True)]
    all_to_all x1 -> x0, blocking collectives: 222 us -> none  [from_experts(): lax.all_to_all(expert_part, 'expert', split_axis=1, concat_axis=1, tiled=...]
    unnamed x28 -> x0, waiting for transfers between devices: 180 us -> none
    dot_general x38 -> x23, matrix products: 236 us -> 78.9 us  [the longest x19 68.8 us: product(): return jnp.einsum(form, left, right, preferred_element_type=jnp.float32)]
    reshape x14 -> x3, local copies, waits for them, and re-layouts: 91.3 us -> 5.01 us  [the longest x1 2.29 us: per_device_gathered(): expanded = expanded.reshape(seq_rows, local_heads, NOPE + VD)]
    all_to_all x3 -> x0, starting transfers between devices: 84.9 us -> none  [the longest x2 45.3 us: to_experts(): lax.all_to_all(gathered, 'expert', split_axis=1, concat_axis=1, tiled=True)]
  transfers between devices with their start and end apart: 25 -> 6, of which waited for: 16 -> 1; matrix products, arithmetic and copies ran while one was open for 19% -> 13% of each run, Pallas kernels for 0% -> 0%
where the time goes in v1:
time: 651 us; the launch traced here: 642 us
  Pallas kernels  483 us (74%)
  matrix products  82.6 us (13%)
  local copies, waits for them, and re-layouts  50.2 us (8%)
  other arithmetic  21.8 us (3%)
    pallas_call x2, Pallas kernels, sum_over_chips(): pl.pallas_call(functools.partial(sum_kernel, tuple(parts), blocks is not...  287 us
    pallas_call x1, Pallas kernels, moe_layer(): pl.pallas_call(moe_kernel, grid=(PLANES, experts), in_specs=[anywhere, wh...  196 us
    dot_general x19, matrix products, product(): return jnp.einsum(form, left, right, preferred_element_type=jnp.float32)  68.8 us
    unnamed x149, local copies, waits for them, and re-layouts  23.2 us
  transfers between devices with their start and end apart: 6, of which 1 were waited for; matrix products, arithmetic and copies ran while one was open for 13% of the time, Pallas kernels for 0%

profile of v1, /device:TPU:0, one launch (start us, length us, event | category | flops | bytes accessed | tf_op | source)
XLA Modules:
  0.0 642.5 jit_solution(4250787626186760443)
XLA Ops:
  12.0 3.3 convolution_convert_fusion.4
  15.3 2.3 copy.176
  17.6 1.9 slice.185
  19.5 5.6 fusion.19
  27.5 3.7 fusion.85
  31.2 2.1 convolution_convert_fusion.7
  41.1 195.6 %shard_map.288 = (bf16[4,2,4,2,128,2176]{5,4,3,2,1,0:T(8,128)(2,1)}, bf16[4,4,128,2048]{3,2,1,0:T(8,128)(2,1)}, bf16[4,4,128,2048]{3,2,1,0:T(8,128)(2,1)}, bf16[...) custom-call(bf16[2,128,2176]{2,1,0:T(8,128)(2,1)} %maximum_maximum_f, ...), custom_call_target="tpu_custom_call" | custom-call | flops 56908316672 | bytes 125829120 | tf_op jit(solution)/shard_map/pallas_call | solution.py:1197
  236.7 165.4 %shard_map.289 = (f32[128,2176]{1,0:T(8,128)}, f32[128,2048]{1,0:T(8,128)}, bf16[16,384,128]{2,1,0:T(8,128)(2,1)}) custom-call(bf16[4,4,128,2176]{3,2,1,0:T(8,128)(2,1)} %get-tuple-element.34.refs_0_, bf16[4,4,128,2176]{3,2,1,0:T(8,128)(2,1)} %get-tuple-element.35.refs_1_, bf16[4,4,128,2048]{3,2,1,0:T(8,128)(2,1)} %get-tuple-element.36.refs_2_, ...), custom_call_target="tpu_custom_call" | custom-call | flops 16220160 | bytes 34603008 | tf_op jit(solution)/shard_map/pallas_call | solution.py:800
  406.2 1.8 multiply_reduce_fusion.1
  411.7 2.4 copy-done.64
  414.2 11.1 %fusion.90 = f32[2,2048,704]{1,2,0:T(8,128)} fusion(bf16[2,1024,2048]{2,1,0:T(8,128)(2,1)S(1)} %copy-done.64, bf16[2,1024,704]{2,1,0:T(8,128)(2,1)} %get-tuple-element.48), kind=kOutput, calls=%fused_computation.193 | convolution fusion | flops 5905580032 | bytes 22806528 | tf_op jit(solution)/shard_map/jsd,jsf->jdf/dot_general | solution.py:427
  425.3 12.2 %fusion.91 = f32[2,2048,704]{1,2,0:T(8,128)} fusion(bf16[2,1024,2048]{2,1,0:T(8,128)(2,1)} %get-tuple-element.47, bf16[2,1024,704]{2,1,0:T(8,128)(2,1)} %get-tuple-element.49), kind=kOutput, calls=%fused_computation.194 | convolution fusion | flops 5905580032 | bytes 22806528 | tf_op jit(solution)/shard_map/jsd,jsf->jdf/dot_general | solution.py:427
  437.6 9.4 %fusion.92 = f32[2,2048,704]{1,2,0:T(8,128)} fusion(bf16[2,1024,2048]{2,1,0:T(8,128)(2,1)S(1)} %bitcast.109, bf16[2,1024,704]{2,1,0:T(8,128)(2,1)S(1)} %copy-done.65), kind=kOutput, calls=%fused_computation.195 | convolution fusion | flops 5905580032 | bytes 22806528 | tf_op jit(solution)/shard_map/jsd,jsf->jdf/dot_general | solution.py:427
  447.9 2.2 copy.164
  450.2 2.2 copy.163
  452.4 2.2 copy.162
  455.2 4.6 convolution_convert_fusion.8
  459.8 2.0 copy.178
  461.9 2.4 fusion.6
  471.4 1.8 fusion.89
  474.8 4.6 convolution_convert_fusion.1
  479.3 5.6 convolution_convert_fusion
  485.0 2.1 convolution_convert_fusion.3
  491.1 3.5 convolution_convert_fusion.2
  494.6 4.4 copy.155
  499.0 3.3 fusion.12
  502.3 3.0 concatenate.74
  505.3 2.0 copy.177
  507.2 1.9 pad.28.clone
  509.2 122.0 %shard_map.290 = (f32[128,1024]{1,0:T(8,128)}, f32[128,1536]{1,0:T(8,128)}, f32[32,2048]{1,0:T(8,128)}, f32[64,576]{1,0:T(8,128)}, f32[64,128]{1,0:T(8,128)}) custom-call(bf16[16,128,1024]{2,1,0:T(8,128)(2,1)} %bitcast.76, bf16[16,128,1536]{2,1,0:T(8,128)(2,1)} %bitcast.75, bf16[16,32,2048]{2,1,0:T(8,128)(2,1)} %bitcast.78, ...), custom_call_target="tpu_custom_call" | custom-call | flops 13148160 | bytes 28049408 | tf_op jit(solution)/shard_map/pallas_call | solution.py:800
  631.2 1.8 fusion.84
  635.1 3.9 fusion.11
  (242 shorter events, 48.1 us)
Async XLA Ops:
  3.3 16.2 %copy-start.3 = (bf16[128,2048]{1,0:T(8,128)(2,1)}, bf16[128,2048]{1,0:T(8,128)(2,1)S(1)}, u32[]{:S(2)}) copy-start(bf16[128,2048]{1,0:T(8,128)(2,1)S(1)} %fusion.7) | copy-start | bytes 1572868
  3.3 16.2 %collective-permute-start.1 = (bf16[128,2048]{1,0:T(8,128)(2,1)S(1)}, bf16[128,2048]{1,0:T(8,128)(2,1)}, u32[]{:S(2)}, u32[]{:S(2)}) collective-permute-start(bf16[128,2048]{1,0:T(8,128)(2,1)S(1)} %fusion.7), channel_id=1, source_target_pairs={{0,1},{1,0},{2,3},{3,2},{4,5},{5,4},{6,7},{7,6},{8,9},{9,8},{10,11... | collective-permute-start | bytes 1572872 | tf_op jit(solution)/shard_map/ppermute | solution.py:423
  3.9 5.2 copy-start.55
  4.7 10.6 %copy-start.5 = (f32[128,576]{0,1:T(8,128)}, f32[128,576]{0,1:T(8,128)S(1)}, u32[]{:S(2)}) copy-start(f32[128,576]{0,1:T(8,128)S(1)} %fusion.87) | copy-start | bytes 884740
  5.8 5.5 collective-permute-start
  9.2 16.8 %copy-start.30 = (f32[256,32]{0,1:T(8,128)}, f32[256,32]{0,1:T(8,128)S(1)}, u32[]{:S(2)}) copy-start(f32[256,32]{0,1:T(8,128)S(1)} %get-tuple-element.167) | copy-start | bytes 98308
  9.2 16.8 %copy-start.32 = (f32[256,32]{0,1:T(8,128)}, f32[256,32]{0,1:T(8,128)S(1)}, u32[]{:S(2)}) copy-start(f32[256,32]{0,1:T(8,128)S(1)} %get-tuple-element.168) | copy-start | bytes 98308
  26.7 4.4 copy-start.40
  27.5 3.7 copy-start.12
  34.0 3.5 copy-start.1
  35.4 2.1 collective-permute-start.2
  409.2 46.0 %collective-permute-start.3 = (bf16[128,2048]{1,0:T(8,128)(2,1)}, bf16[128,2048]{1,0:T(8,128)(2,1)}, u32[]{:S(2)}, u32[]{:S(2)}) collective-permute-start(bf16[128,2048]{1,0:T(8,128)(2,1)} %fusion.80), channel_id=1, source_target_pairs={{0,1},{1,0},{2,3},{3,2},{4,5},{5,4},{6,7},{7,6},{8,9},{9,8},{10,11... | collective-permute-start | bytes 1572872 | tf_op jit(solution)/shard_map/ppermute | solution.py:423
  410.0 4.2 copy-start.64
  414.2 23.4 %slice-start.2 = ((s8[8388608]{0:T(1024)(128)(4,1)}), s8[4194304]{0:T(1024)(128)(4,1)S(1)}, s32[]{:S(2)}) async-start(s8[8388608]{0:T(1024)(128)(4,1)} %bitcast.108), calls=%async_computation.2 | async-start | bytes 8388608
  425.3 12.3 %slice-start.3 = ((s8[8388608]{0:T(1024)(128)(4,1)}), s8[4194304]{0:T(1024)(128)(4,1)S(1)}, s32[]{:S(2)}) async-start(s8[8388608]{0:T(1024)(128)(4,1)} %bitcast.108), calls=%async_computation.3 | async-start | bytes 8388608
  425.3 12.3 %copy-start.65 = (bf16[2,1024,704]{2,1,0:T(8,128)(2,1)S(1)}, bf16[2,1024,704]{2,1,0:T(8,128)(2,1)}, u32[]{:S(2)}) copy-start(bf16[2,1024,704]{2,1,0:T(8,128)(2,1)} %get-tuple-element.51) | copy-start | bytes 8650756
  437.5 9.5 %copy-start.10 = (bf16[128,2048]{1,0:T(8,128)(2,1)S(1)}, bf16[128,2048]{1,0:T(8,128)(2,1)}, u32[]{:S(2)}) copy-start(bf16[128,2048]{1,0:T(8,128)(2,1)} %copy-done.9) | copy-start | bytes 1572868
  455.2 6.6 %copy-start.52 = (f32[8,256]{1,0:T(8,128)S(1)}, f32[8,256]{1,0:T(8,128)}, u32[]{:S(2)}) copy-start(f32[8,256]{1,0:T(8,128)} %copy-done.51) | copy-start | bytes 24580
  464.6 6.7 %slice-start = ((s8[6291456]{0:T(1024)(128)(4,1)}), s8[4194304]{0:T(1024)(128)(4,1)S(1)}, s32[]{:S(2)}) async-start(s8[6291456]{0:T(1024)(128)(4,1)} %bitcast.103), calls=%async_computation | async-start | bytes 8388608
  466.5 4.8 slice-start.1
  470.7 16.3 %collective-permute-start.5 = (bf16[128,576]{0,1:T(8,128)(2,1)S(1)}, bf16[128,576]{0,1:T(8,128)(2,1)S(1)}, u32[]{:S(2)}, u32[]{:S(2)}) collective-permute-start(bf16[128,576]{0,1:T(8,128)(2,1)S(1)} %fusion.28), channel_id=1, source_target_pairs={{0,1},{1,0},{2,3},{3,2},{4,5},{5,4},{6,7},{7,6},{8,9},{9,8},{10,11... | collective-permute-start | bytes 442376 | tf_op jit(solution)/shard_map/ppermute | solution.py:423
  474.2 5.2 copy-start.4
  474.2 24.8 %collective-permute-start.4 = (bf16[128,2048]{1,0:T(8,128)(2,1)}, bf16[128,2048]{1,0:T(8,128)(2,1)}, u32[]{:S(2)}, u32[]{:S(2)}) collective-permute-start(bf16[128,2048]{1,0:T(8,128)(2,1)} %slice.273), channel_id=1, source_target_pairs={{0,1},{1,0},{2,3},{3,2},{4,5},{5,4},{6,7},{7,6},{8,9},{9,8},{10,11... | collective-permute-start | bytes 1572872 | tf_op jit(solution)/shard_map/ppermute | solution.py:423
  479.3 5.6 copy-start.15
  494.6 4.4 copy-start.43
  509.2 125.9 %copy-start.37 = (f32[2048]{0:T(1024)S(1)}, f32[2048]{0:T(1024)}, u32[]{:S(2)}) copy-start(f32[2048]{0:T(1024)} %param.24) | copy-start | bytes 24580
  509.2 125.9 %copy-start.50 = (f32[128]{0:T(128)S(1)}, f32[128]{0:T(128)}, u32[]{:S(2)}) copy-start(f32[128]{0:T(128)} %copy-done.48) | copy-start | bytes 1540
  509.2 125.9 %copy-start.54 = (f32[128]{0:T(128)S(1)}, f32[128]{0:T(128)}, u32[]{:S(2)}) copy-start(f32[128]{0:T(128)} %copy-done.53) | copy-start | bytes 1540
  509.2 125.9 %copy-start.61 = (f32[128]{0:T(128)S(1)}, f32[128]{0:T(128)}, u32[]{:S(2)}) copy-start(f32[128]{0:T(128)} %copy-done.60) | copy-start | bytes 1540
  635.1 3.9 copy-start.21
  635.1 4.8 copy-start.38
  635.1 5.4 copy-start.34
  (44 other events, 81.2 us)

commit v2 on v1

--- a/solution.py
+++ b/solution.py
@@ -421,6 +421,20 @@
 
 def send_core(values):
     return lax.ppermute(values, TENSOR, [(0, 1), (1, 0)])
+
+
+def chip_pairs(move):
+    chips = [(z, y, x) for z in range(PLANES) for y in range(2) for x in range(2)]
+    moved = [move(*chip) for chip in chips]
+    return [tuple((z * 2 + y) * 2 + x for z, y, x in pair) for pair in zip(chips, moved)]
+
+
+def send_x(values):
+    return lax.ppermute(values, EXPERT, chip_pairs(lambda z, y, x: (z, y, 1 - x)))
+
+
+def send_y(values):
+    return lax.ppermute(values, EXPERT, chip_pairs(lambda z, y, x: (z, 1 - y, x)))
 
 
 def product(form, left, right):
@@ -827,6 +841,7 @@
 
 
 def moe_kernel(own_rows_in, lanes, w_gate, w_up, w_down, sw_gate, sw_up, sw_down, *refs):
+    near, refs = refs[:3], refs[3:]
     land, out_mine, out_other, grad_mine, grad_other = refs[:5]
     rows_out, pairs_out, hidden_out, gate_out, up_out, shared_out = refs[5:11]
     rows_kept, grads_kept, out_kept, back_kept, extra_kept, s_hidden, s_grads, seats = refs[11:19]
@@ -883,6 +898,31 @@
             device_id_type=MESH,
         )
 
+    def near_sides():
+        own = own_rows_in.at[0]
+        return [
+            remote(0, 0, own, land.at[0, 0, 1, 0], chips.to_x),
+            remote(0, 1, own, land.at[0, 0, 2, 0], chips.to_y),
+        ]
+
+    def near_corners():
+        half = land.shape[4] // 2
+        ends = (slice(0, half), slice(half, 2 * half))
+        return [
+            remote(0, 2 + k, land.at[0, 0, 1 + k, 0, rows], land.at[0, 0, 3, 0, rows], to)
+            for k, (rows, to) in enumerate(zip(ends, (chips.to_y, chips.to_x)))
+        ]
+
+    def near_core(place):
+        source = land.at[0, 0, place, 0]
+        return remote(0, 4 + place, source, land.at[0, 1, place, 0], chips.to_core)
+
+    def near_cores_at_once():
+        own = remote(0, 4, own_rows_in, land.at[0, 1, 0], chips.to_core)
+        return [own] + [
+            remote(0, 8 + k, near[k], land.at[0, 1, 1 + k, 1], chips.to_core) for k in range(3)
+        ]
+
     def start_plane(step):
         for copy in side_copies(step) + [core_copy(step, 0)]:
             copy.start()
@@ -931,7 +971,8 @@
         greet(
             [chips.to_x, chips.to_y, chips.to_core, chips.to_z(1), chips.to_z(PLANES - 1)]
         )
-        start_plane(0)
+        for copy in near_sides() + near_cores_at_once():
+            copy.start()
         z_copy(1).start()
 
         @pl.when(shared_here)
@@ -942,7 +983,10 @@
         for expert in range(experts):
             for copy in weight_copies(expert):
                 copy.start()
-        pass_corners(0)
+        for copy in near_sides():
+            copy.wait_recv()
+        for copy in near_corners() + [near_core(1), near_core(2)]:
+            copy.start()
         z_copy(1).wait_recv()
         z_copy(2).start()
         start_plane(1)
@@ -957,7 +1001,11 @@
             s_in[...] = jnp.zeros(s_in.shape, low)
             s_down[...] = jnp.zeros(s_down.shape, low)
 
-        finish_plane(0)
+        for copy in near_corners():
+            copy.wait_recv()
+        near_core(3).start()
+        for copy in near_cores_at_once() + [near_core(place) for place in (1, 2, 3)]:
+            copy.wait_recv()
 
     def pair_place(pair):
         return pair // (pairs // 2), slice((pair % (pairs // 2)) * 2, (pair % (pairs // 2)) * 2 + 2)
@@ -993,9 +1041,13 @@
         return here[2 * pair : 2 * pair + 2, :, :columns].reshape(pair_rows_all, columns)
 
     def own_coming():
-        for which, here in enumerate((x_here, g_here)):
-            for block, source in enumerate((own_rows_in.at[which], land.at[0, 0, 1, which])):
-                yield pltpu.make_async_copy(source, here.at[block], come.at[which * pairs])
+        rows = [own_rows_in.at[0]] + [land.at[0, 0, place, 0] for place in (1, 2, 3)]
+        grads = [own_rows_in.at[1], *near]
+        for which, (here, sources) in enumerate(((x_here, rows), (g_here, grads))):
+            for block, source in enumerate(sources):
+                yield pltpu.make_async_copy(
+                    source, here.at[block], come.at[which * pairs + block // 2]
+                )
 
     @pl.when((step == 0) & (plane == 0))
     def _():
@@ -1004,12 +1056,13 @@
 
     @pl.when((step == 0) & (plane > 0))
     def _():
-        for copy in coming(0):
-            copy.start()
+        for pair in range(pairs // 2):
+            for copy in coming(pair):
+                copy.start()
 
     @pl.when(step == 0)
     def _():
-        for pair in range(1, pairs):
+        for pair in range(pairs // 2, pairs):
             for copy in coming(pair):
                 copy.start()
         tokens = lax.broadcasted_iota(jnp.int32, (pair_rows_all, pair_rows_all), 0)
@@ -1161,7 +1214,11 @@
         for k in range(1, PLANES):
             z_copy(k).wait_send()
 
-        @pl.loop(0, PLANES)
+        near_cores = near_cores_at_once() + [near_core(place) for place in (1, 2, 3)]
+        for copy in near_sides() + near_corners() + near_cores:
+            copy.wait_send()
+
+        @pl.loop(1, PLANES)
         def _(sent):
             for copy in side_copies(sent) + corner_copies(sent):
                 copy.wait_send()
@@ -1169,7 +1226,7 @@
                 core_copy(sent, k).wait_send()
 
 
-def moe_layer(own_rows_in, lanes, weights):
+def moe_layer(own_rows_in, near, lanes, weights):
     experts, units, width = weights[0].shape
     _, own_rows, wide = own_rows_in.shape
     blocks, pairs, pair_rows, pair_slots = 4, 4, 2 * own_rows, EXTRA
@@ -1192,12 +1249,12 @@
         for columns in (width, width, units, units, units)
     ]
     shared = [jax.ShapeDtypeStruct((chips, 3 * half, width // chips), low)]
-    operands = [own_rows_in, lanes] + list(weights)
+    operands = [own_rows_in, lanes] + list(weights) + near
     work = 2 * tokens * width * (8 * half + 2 * pair_slots) + 12 * experts * slots * width * units
     results = pl.pallas_call(
         moe_kernel,
         grid=(PLANES, experts),
-        in_specs=[anywhere, whole(lanes)] + [anywhere] * len(weights),
+        in_specs=[anywhere, whole(lanes)] + [anywhere] * (len(weights) + len(near)),
         out_specs=[anywhere] * 5
         + [pl.BlockSpec((1, slots, v.shape[2]), lambda s, j: (j, s, 0)) for v in keep]
         + [whole(v) for v in shared],
@@ -1223,8 +1280,8 @@
             pltpu.SemaphoreType.DMA((2 * pairs,)),
             pltpu.SemaphoreType.DMA((2 * pairs,)),
             pltpu.SemaphoreType.DMA((experts + 1, 3)),
-            pltpu.SemaphoreType.DMA((PLANES, 9)),
-            pltpu.SemaphoreType.DMA((PLANES, 9)),
+            pltpu.SemaphoreType.DMA((PLANES, 11)),
+            pltpu.SemaphoreType.DMA((PLANES, 11)),
             pltpu.SemaphoreType.DMA((PLANES,)),
             pltpu.SemaphoreType.DMA((PLANES,)),
         ],
@@ -1236,6 +1293,34 @@
         ),
     )(*operands)
     return results[1:3], results[3:5], results[5:]
+
+
+def expert_grads_kernel(rows, pair_grads, grad_gate, grad_up, hidden, for_gate, for_up, for_down):
+    for_gate[0] = dot_tn(grad_gate[0], rows[0])
+    for_up[0] = dot_tn(grad_up[0], rows[0])
+    for_down[0] = dot_tn(hidden[0], pair_grads[0])
+
+
+def expert_grads(rows, pair_grads, grad_gate, grad_up, hidden):
+    experts, slots, width = rows.shape
+    units = hidden.shape[2]
+    columns = width // 2
+    of_columns = pl.BlockSpec((1, slots, columns), lambda j, c: (j, 0, c))
+    of_units = pl.BlockSpec((1, slots, units), lambda j, c: (j, 0, 0))
+    grads = pl.pallas_call(
+        expert_grads_kernel,
+        grid=(experts, width // columns),
+        in_specs=[of_columns] * 2 + [of_units] * 3,
+        out_specs=[pl.BlockSpec((1, units, columns), lambda j, c: (j, 0, c))] * 3,
+        out_shape=[jax.ShapeDtypeStruct((experts, units, width), jnp.float32)] * 3,
+        compiler_params=pltpu.CompilerParams(vmem_limit_bytes=VMEM_LIMIT),
+        cost_estimate=pl.CostEstimate(
+            flops=6 * experts * slots * width * units,
+            bytes_accessed=60 << 20,
+            transcendentals=0,
+        ),
+    )(rows, pair_grads, grad_gate, grad_up, hidden)
+    return [jnp.swapaxes(grad, 1, 2) for grad in grads]
 
 
 def per_device_gathered(
@@ -1270,6 +1355,10 @@
     capacity = own_rows * TOPK * 4 // (3 * experts)
     scale = 1.0 / math.sqrt(NOPE + ROPE)
 
+    beside = jnp.pad(routes.astype(jnp.bfloat16), ((0, 0), (0, EXTRA - TOPK)))
+    block = jnp.concatenate([cotangent, beside], axis=1)
+    from_x, from_y = send_x(block), send_y(block)
+
     flat_in = inputs.astype(jnp.float32)
     scale_one = lax.rsqrt(jnp.mean(flat_in * flat_in, axis=-1, keepdims=True) + EPS)
     normed_one = flat_in * scale_one
@@ -1290,6 +1379,8 @@
         return jnp.concatenate([values, send_core(values)], axis=0)
 
     h_all = both(h_own)
+    h_all, from_x, from_y = lax.optimization_barrier((h_all, from_x, from_y))
+    near = [from_x, from_y, send_y(from_x)]
     lat_rope = both(jnp.concatenate([lat_own, rope_own], axis=1))
     lat_all, rope_all = lat_rope[:, :LATENT], lat_rope[:, LATENT:]
     cos_all, sin_all = rope_tables(places_all, ROPE)
@@ -1334,16 +1425,9 @@
     raised = jnp.where(chosen, jnp.exp(masked - jnp.max(masked, axis=-1, keepdims=True)), 0.0)
     gates = raised / jnp.sum(raised, axis=-1, keepdims=True)
     high_gates = lax.reduce_precision(gates, 8, 7)
-    beside = jnp.stack(
-        [
-            jnp.pad(
-                jnp.concatenate([high_gates, gates - high_gates], axis=1),
-                ((0, 0), (0, EXTRA - 2 * experts)),
-            ),
-            jnp.pad(routes.astype(jnp.float32), ((0, 0), (0, EXTRA - TOPK))),
-        ]
-    ).astype(jnp.bfloat16)
-    own_rows_in = jnp.concatenate([jnp.stack([h_moe, cotangent]), beside], axis=2)
+    beside = [high_gates.astype(jnp.bfloat16), (gates - high_gates).astype(jnp.bfloat16)]
+    beside.append(jnp.zeros((own_rows, EXTRA - 2 * experts), jnp.bfloat16))
+    own_rows_in = jnp.stack([jnp.concatenate([h_moe, *beside], axis=1), block])
 
     own_ids = expert_index * local_experts + jnp.arange(local_experts, dtype=jnp.int32)
     lane_ids = jnp.arange(EXTRA, dtype=jnp.int32)[None, :]
@@ -1357,7 +1441,7 @@
 
     all_weights = tuple(jnp.swapaxes(w, 1, 2) for w in (w_expert_gate, w_expert_up, w_expert_down))
     all_weights += (w_shared_gate, w_shared_up, w_shared_down)
-    out_parts, grad_parts, kept = moe_layer(own_rows_in, lanes, all_weights)
+    out_parts, grad_parts, kept = moe_layer(own_rows_in, near, lanes, all_weights)
     shared_grads = kept[5].reshape((PLANES, 2, 2) + kept[5].shape[1:])
     moe_back, moe_out, shared_grads = sum_over_chips(
         1, [(2, grad_parts, 512), (2, out_parts, 512)], shared_grads
@@ -1454,9 +1538,9 @@
     grad_norm_latent = (small[:, experts + 4] + small[:, experts + 5])[:gain_rows]
 
     rows, pair_grads, hidden, grad_gate, grad_up = kept[:5]
-    grad_expert_down = product("jsd,jsf->jdf", pair_grads, hidden)
-    grad_expert_gate = product("jsd,jsf->jdf", rows, grad_gate)
-    grad_expert_up = product("jsd,jsf->jdf", rows, grad_up)
+    grad_expert_gate, grad_expert_up, grad_expert_down = expert_grads(
+        rows, pair_grads, grad_gate, grad_up, hidden
+    )
     columns = w_shared_gate.shape[1]
     shared_grads = shared_grads[: columns // EXTRA].reshape(-1, 3, EXTRA, share)
     shared_grads = (

time: 651 us -> 626 us (0.962)
  matrix products: 82.6 us -> 49.6 us
  local copies, waits for them, and re-layouts: 50.2 us -> 39.8 us
  waiting for transfers between devices: 0.84 us -> 7.99 us
    dot_general x19 -> x16, matrix products: 68.8 us -> 35.1 us  [product(): return jnp.einsum(form, left, right, preferred_element_type=jnp.float32)]
    pallas_call x0 -> x1, Pallas kernels: none -> 28 us  [expert_grads(): pl.pallas_call(expert_grads_kernel, grid=(experts, width // columns), in_...]
    pallas_call x1, Pallas kernels: 196 us -> 173 us  [moe_layer(): pl.pallas_call(moe_kernel, grid=(PLANES, experts), in_specs=[anywhere, wh...]
    ppermute x0 -> x3, waiting for transfers between devices: none -> 7.37 us  [the longest x2 7.37 us: send_y(): lax.ppermute(values, EXPERT, chip_pairs(lambda z, y, x: (z, 1 - y, x)))]
    unnamed x149 -> x141, local copies, waits for them, and re-layouts: 23.2 us -> 18.2 us
  transfers between devices with their start and end apart: 6 -> 9, of which waited for: 1 -> 2; matrix products, arithmetic and copies ran while one was open for 13% -> 7% of each run, Pallas kernels for 0% -> 5%
where the time goes in v2:
time: 626 us; the launch traced here: 618 us
  Pallas kernels  488 us (78%)
  matrix products  49.6 us (8%)
  local copies, waits for them, and re-layouts  39.8 us (6%)
  other arithmetic  23.7 us (4%)
  waiting for transfers between devices  7.99 us (1%)
  starting transfers between devices  7.19 us (1%)
    pallas_call x2, Pallas kernels, sum_over_chips(): pl.pallas_call(functools.partial(sum_kernel, tuple(parts), blocks is not...  287 us
    pallas_call x1, Pallas kernels, moe_layer(): pl.pallas_call(moe_kernel, grid=(PLANES, experts), in_specs=[anywhere, wh...  173 us
    dot_general x16, matrix products, product(): return jnp.einsum(form, left, right, preferred_element_type=jnp.float32)  35.1 us
    pallas_call x1, Pallas kernels, expert_grads(): pl.pallas_call(expert_grads_kernel, grid=(experts, width // columns), in_...  28 us
    unnamed x141, local copies, waits for them, and re-layouts  18.2 us
  transfers between devices with their start and end apart: 9, of which 2 were waited for; matrix products, arithmetic and copies ran while one was open for 7% of the time, Pallas kernels for 5%

profile of v2, /device:TPU:0, one launch (start us, length us, event | category | flops | bytes accessed | tf_op | source)
XLA Modules:
  0.0 617.9 jit_solution(7593201997403115251)
XLA Ops:
  1.7 2.1 fusion.75
  3.8 3.0 collective-permute-start.3
  6.7 1.5 collective-permute-start.2
  16.5 3.3 convolution_convert_fusion.4
  19.8 2.2 copy.158
  22.0 1.9 slice.185
  25.1 5.8 fusion.84
  33.2 4.3 fusion.81
  37.5 2.1 convolution_convert_fusion.7
  46.4 1.9 concatenate.66
  48.3 2.3 pad_maximum_fusion.own_rows_in
  50.6 7.4 %collective-permute-done.5.refs_2_ = bf16[128,2176]{1,0:T(8,128)(2,1)} collective-permute-done((bf16[128,2176]{1,0:T(8,128)(2,1)}, bf16[128,2176]{1,0:T(8,128)(2,1)}, u32[]{:S(2)}, u32[]{:S(2)}) %collective-permute-start.5) | collective-permute-done | bytes 557088 | tf_op jit(solution)/shard_map/ppermute | solution.py:437
  58.0 172.9 %shard_map.288 = (bf16[4,2,4,2,128,2176]{5,4,3,2,1,0:T(8,128)(2,1)}, bf16[4,4,128,2048]{3,2,1,0:T(8,128)(2,1)}, bf16[4,4,128,2048]{3,2,1,0:T(8,128)(2,1)}, bf16[...) custom-call(bf16[2,128,2176]{2,1,0:T(8,128)(2,1)} %pad_maximum_fusio, ...), custom_call_target="tpu_custom_call" | custom-call | flops 56908316672 | bytes 125829120 | tf_op jit(solution)/shard_map/pallas_call | solution.py:1254
  230.9 163.6 %shard_map.289 = (f32[128,2176]{1,0:T(8,128)}, f32[128,2048]{1,0:T(8,128)}, bf16[16,384,128]{2,1,0:T(8,128)(2,1)}) custom-call(bf16[4,4,128,2176]{3,2,1,0:T(8,128)(2,1)} %get-tuple-element.43.refs_0_, bf16[4,4,128,2176]{3,2,1,0:T(8,128)(2,1)} %get-tuple-element.44.refs_1_, bf16[4,4,128,2048]{3,2,1,0:T(8,128)(2,1)} %get-tuple-element.45.refs_2_, ...), custom_call_target="tpu_custom_call" | custom-call | flops 16220160 | bytes 34603008 | tf_op jit(solution)/shard_map/pallas_call | solution.py:814
  398.6 1.9 multiply_reduce_fusion.1
  400.6 1.7 fusion.76
  405.1 28.0 %shard_map.291 = (f32[2,704,2048]{2,1,0:T(8,128)}, f32[2,704,2048]{2,1,0:T(8,128)}, f32[2,704,2048]{2,1,0:T(8,128)}) custom-call(bf16[2,1024,2048]{2,1,0:T(8,128)(2,1)} %get-tuple-element.56.rows, bf16[2,1024,2048]{2,1,0:T(8,128)(2,1)} %get-tuple-element.57.pair_grads, bf16[2,1024,704]{2,1,0:T(8,128)(2,1)} %get-tuple-element.58.grad_gate, ...), custom_call_target="tpu_custom_call" | custom-call | flops 17716740096 | bytes 62914560 | tf_op jit(solution)/shard_map/pallas_call | solution.py:1310
  433.4 2.2 copy.149
  435.7 2.2 copy.148
  439.6 3.8 convolution_convert_fusion.8
  443.7 2.2 fusion.6
  449.9 4.7 fusion.86
  454.6 4.5 convolution_convert_fusion
  459.2 1.5 copy-done.19
  461.8 4.6 convolution_convert_fusion.1
  466.4 2.1 convolution_convert_fusion.3
  470.5 2.4 convolution_convert_fusion.2
  472.9 4.4 copy.143
  477.3 3.2 fusion.13
  484.5 123.1 %shard_map.290 = (f32[128,1024]{1,0:T(8,128)}, f32[128,1536]{1,0:T(8,128)}, f32[32,2048]{1,0:T(8,128)}, f32[64,576]{1,0:T(8,128)}, f32[64,128]{1,0:T(8,128)}) custom-call(bf16[16,128,1024]{2,1,0:T(8,128)(2,1)} %bitcast.71, bf16[16,128,1536]{2,1,0:T(8,128)(2,1)} %bitcast.70, bf16[16,32,2048]{2,1,0:T(8,128)(2,1)} %bitcast.73, ...), custom_call_target="tpu_custom_call" | custom-call | flops 13148160 | bytes 28049408 | tf_op jit(solution)/shard_map/pallas_call | solution.py:814
  607.6 1.8 fusion.80
  611.5 2.9 fusion.12
  (237 shorter events, 44.4 us)
Async XLA Ops:
  0.6 9.5 %copy-start = (bf16[2048,576]{0,1:T(8,128)(2,1)S(1)}, bf16[2048,576]{0,1:T(8,128)(2,1)}, u32[]{:S(2)}) copy-start(bf16[2048,576]{0,1:T(8,128)(2,1)} %param.20) | copy-start | bytes 7077892
  0.7 8.8 %copy-start.1 = (bf16[128,2048]{1,0:T(8,128)(2,1)S(1)}, bf16[128,2048]{1,0:T(8,128)(2,1)}, u32[]{:S(2)}) copy-start(bf16[128,2048]{1,0:T(8,128)(2,1)} %param.17) | copy-start | bytes 1572868
  0.7 8.8 %copy-start.42 = (f32[2048]{0:T(1024)S(1)}, f32[2048]{0:T(1024)}, u32[]{:S(2)}) copy-start(f32[2048]{0:T(1024)} %param.18) | copy-start | bytes 24580
  3.8 21.3 %collective-permute-start.3 = (bf16[128,2176]{1,0:T(8,128)(2,1)}, bf16[128,2176]{1,0:T(8,128)(2,1)}, u32[]{:S(2)}, u32[]{:S(2)}) collective-permute-start(bf16[128,2176]{1,0:T(8,128)(2,1)} %get-tuple-element.167), channel_id=1, source_target_pairs={{0,4},{2,6},{4,0},{6,2},{8,12},{10,14},{12,8},{14,10},{16,20},{18,... | collective-permute-start | bytes 1671176 | tf_op jit(solution)/shard_map/ppermute | solution.py:437
  6.7 18.3 %collective-permute-start.2 = (bf16[128,2176]{1,0:T(8,128)(2,1)}, bf16[128,2176]{1,0:T(8,128)(2,1)}, u32[]{:S(2)}, u32[]{:S(2)}) collective-permute-start(bf16[128,2176]{1,0:T(8,128)(2,1)} %get-tuple-element.167), channel_id=1, source_target_pairs={{0,2},{2,0},{4,6},{6,4},{8,10},{10,8},{12,14},{14,12},{16,18},{18,... | collective-permute-start | bytes 1671176 | tf_op jit(solution)/shard_map/ppermute | solution.py:433
  10.1 13.8 %copy-start.6 = (bf16[128,2048]{1,0:T(8,128)(2,1)}, bf16[128,2048]{1,0:T(8,128)(2,1)S(1)}, u32[]{:S(2)}) copy-start(bf16[128,2048]{1,0:T(8,128)(2,1)S(1)} %fusion.8) | copy-start | bytes 1572868
  10.1 13.8 %collective-permute-start.1 = (bf16[128,2048]{1,0:T(8,128)(2,1)S(1)}, bf16[128,2048]{1,0:T(8,128)(2,1)}, u32[]{:S(2)}, u32[]{:S(2)}) collective-permute-start(bf16[128,2048]{1,0:T(8,128)(2,1)S(1)} %fusion.8), channel_id=1, source_target_pairs={{0,1},{1,0},{2,3},{3,2},{4,5},{5,4},{6,7},{7,6},{8,9},{9,8},{10,11... | collective-permute-start | bytes 1572872 | tf_op jit(solution)/shard_map/ppermute | solution.py:423
  11.8 3.9 collective-permute-start
  13.3 18.5 %copy-start.31 = (f32[256,32]{0,1:T(8,128)}, f32[256,32]{0,1:T(8,128)S(1)}, u32[]{:S(2)}) copy-start(f32[256,32]{0,1:T(8,128)S(1)} %get-tuple-element.182) | copy-start | bytes 98308
  13.3 18.5 %copy-start.33 = (f32[256,32]{0,1:T(8,128)}, f32[256,32]{0,1:T(8,128)S(1)}, u32[]{:S(2)}) copy-start(f32[256,32]{0,1:T(8,128)S(1)} %get-tuple-element.183) | copy-start | bytes 98308
  25.0 5.9 copy-start.8
  32.5 5.0 copy-start.37
  33.2 4.3 copy-start.13
  41.8 2.0 collective-permute-start.4
  42.7 15.3 %collective-permute-start.5 = (bf16[128,2176]{1,0:T(8,128)(2,1)}, bf16[128,2176]{1,0:T(8,128)(2,1)}, u32[]{:S(2)}, u32[]{:S(2)}) collective-permute-start(bf16[128,2176]{1,0:T(8,128)(2,1)} %collective-permute-done.2.refs_0_), channel_id=1, source_target_pairs={{0,4},{2,6},{4,0},{6,2},{8,12},{10,14},{12,8},{14,10},{16,20},{18,... | collective-permute-start | bytes 1671176 | tf_op jit(solution)/shard_map/ppermute | solution.py:437
  402.3 37.3 %collective-permute-start.6 = (bf16[128,2048]{1,0:T(8,128)(2,1)}, bf16[128,2048]{1,0:T(8,128)(2,1)}, u32[]{:S(2)}, u32[]{:S(2)}) collective-permute-start(bf16[128,2048]{1,0:T(8,128)(2,1)} %get-tuple-element.152), channel_id=1, source_target_pairs={{0,1},{1,0},{2,3},{3,2},{4,5},{5,4},{6,7},{7,6},{8,9},{9,8},{10,11... | collective-permute-start | bytes 1572872 | tf_op jit(solution)/shard_map/ppermute | solution.py:423
  405.1 28.1 %copy-start.5 = (bf16[128,2048]{1,0:T(8,128)(2,1)S(1)}, bf16[128,2048]{1,0:T(8,128)(2,1)}, u32[]{:S(2)}) copy-start(bf16[128,2048]{1,0:T(8,128)(2,1)} %copy-done.4) | copy-start | bytes 1572868
  439.6 4.0 copy-start.48
  449.9 4.7 copy-start.9
  454.6 13.8 %copy-start.21 = (f32[256,2048]{1,0:T(8,128)}, f32[256,2048]{1,0:T(8,128)S(1)}, u32[]{:S(2)}) copy-start(f32[256,2048]{1,0:T(8,128)S(1)} %fusion.86) | copy-start | bytes 6291460
  461.5 4.9 copy-start.16
  461.5 8.1 %collective-permute-start.8 = (bf16[128,576]{0,1:T(8,128)(2,1)S(1)}, bf16[128,576]{0,1:T(8,128)(2,1)S(1)}, u32[]{:S(2)}, u32[]{:S(2)}) collective-permute-start(bf16[128,576]{0,1:T(8,128)(2,1)S(1)} %fusion.29), channel_id=1, source_target_pairs={{0,1},{1,0},{2,3},{3,2},{4,5},{5,4},{6,7},{7,6},{8,9},{9,8},{10,11... | collective-permute-start | bytes 442376 | tf_op jit(solution)/shard_map/ppermute | solution.py:423
  469.3 8.0 %collective-permute-start.7 = (bf16[128,2048]{1,0:T(8,128)(2,1)}, bf16[128,2048]{1,0:T(8,128)(2,1)}, u32[]{:S(2)}, u32[]{:S(2)}) collective-permute-start(bf16[128,2048]{1,0:T(8,128)(2,1)} %slice.279), channel_id=1, source_target_pairs={{0,1},{1,0},{2,3},{3,2},{4,5},{5,4},{6,7},{7,6},{8,9},{9,8},{10,11... | collective-permute-start | bytes 1572872 | tf_op jit(solution)/shard_map/ppermute | solution.py:423
  472.9 4.4 copy-start.3
  472.9 4.4 copy-start.43
  472.9 4.5 copy-start.50
  477.3 3.7 copy-start.44
  484.5 127.0 %copy-start.51 = (f32[128]{0:T(128)S(1)}, f32[128]{0:T(128)}, u32[]{:S(2)}) copy-start(f32[128]{0:T(128)} %copy-done.49) | copy-start | bytes 1540
  484.5 127.0 %copy-start.61 = (f32[128]{0:T(128)S(1)}, f32[128]{0:T(128)}, u32[]{:S(2)}) copy-start(f32[128]{0:T(128)} %broadcast_multiply_fusion.1) | copy-start | bytes 1540
  610.9 3.6 copy-start.24
  611.5 3.8 copy-start.36
  611.5 4.5 copy-start.35
  (43 other events, 81.8 us)

commit v3 on v2

--- a/solution.py
+++ b/solution.py
@@ -1409,6 +1409,7 @@
     probs = weights / jnp.sum(weights, axis=-1, keepdims=True)
     attended = product("hqk,khd->qhd", probs.astype(jnp.bfloat16), value)
     attended_flat = attended.astype(jnp.bfloat16).reshape(seq_rows, local_heads * VD)
+    attended_flat, near = lax.optimization_barrier((attended_flat, near))
     attn_terms = product("sv,dv->sd", attended_flat, w_output)
     after_attn = (
         flat_in

time: 626 us -> 636 us (1.016)
  local copies, waits for them, and re-layouts: 39.8 us -> 48.2 us
    ppermute x2, waiting for transfers between devices: 7.37 us -> 0.75 us  [send_y(): lax.ppermute(values, EXPERT, chip_pairs(lambda z, y, x: (z, 1 - y, x)))]
    unnamed x141 -> x143, local copies, waits for them, and re-layouts: 18.2 us -> 19.4 us
  transfers between devices with their start and end apart: 9 -> 9, of which waited for: 2 -> 2; matrix products, arithmetic and copies ran while one was open for 7% -> 10% of each run, Pallas kernels for 5% -> 4%
where the time goes in v3:
time: 636 us; the launch traced here: 627 us
  Pallas kernels  491 us (77%)
  matrix products  51.3 us (8%)
  local copies, waits for them, and re-layouts  48.2 us (8%)
  other arithmetic  26.1 us (4%)
  starting transfers between devices  7.1 us (1%)
    pallas_call x2, Pallas kernels, sum_over_chips(): pl.pallas_call(functools.partial(sum_kernel, tuple(parts), blocks is not...  291 us
    pallas_call x1, Pallas kernels, moe_layer(): pl.pallas_call(moe_kernel, grid=(PLANES, experts), in_specs=[anywhere, wh...  172 us
    dot_general x16, matrix products, product(): return jnp.einsum(form, left, right, preferred_element_type=jnp.float32)  37.8 us
    pallas_call x1, Pallas kernels, expert_grads(): pl.pallas_call(expert_grads_kernel, grid=(experts, width // columns), in_...  28 us
    unnamed x143, local copies, waits for them, and re-layouts  19.4 us
  transfers between devices with their start and end apart: 9, of which 2 were waited for; matrix products, arithmetic and copies ran while one was open for 10% of the time, Pallas kernels for 4%

profile of v3, /device:TPU:0, one launch (start us, length us, event | category | flops | bytes accessed | tf_op | source)
XLA Modules:
  0.0 627.4 jit_solution(4623614412507756677)
XLA Ops:
  1.7 2.1 fusion.75
  3.8 3.0 collective-permute-start.3
  18.4 3.3 convolution_convert_fusion.4
  21.7 2.3 copy.158
  24.0 1.9 slice.185
  27.6 5.5 fusion.84
  35.4 3.7 fusion.81
  39.1 2.1 convolution_convert_fusion.7
  48.0 1.9 concatenate.66
  49.9 2.3 pad_maximum_fusion.own_rows_in
  52.2 172.0 %shard_map.288 = (bf16[4,2,4,2,128,2176]{5,4,3,2,1,0:T(8,128)(2,1)}, bf16[4,4,128,2048]{3,2,1,0:T(8,128)(2,1)}, bf16[4,4,128,2048]{3,2,1,0:T(8,128)(2,1)}, bf16[...) custom-call(bf16[2,128,2176]{2,1,0:T(8,128)(2,1)} %pad_maximum_fusio, ...), custom_call_target="tpu_custom_call" | custom-call | flops 56908316672 | bytes 125829120 | tf_op jit(solution)/shard_map/pallas_call | solution.py:1254
  224.2 165.5 %shard_map.289 = (f32[128,2176]{1,0:T(8,128)}, f32[128,2048]{1,0:T(8,128)}, bf16[16,384,128]{2,1,0:T(8,128)(2,1)}) custom-call(bf16[4,4,128,2176]{3,2,1,0:T(8,128)(2,1)} %get-tuple-element.51.refs_0_, bf16[4,4,128,2176]{3,2,1,0:T(8,128)(2,1)} %get-tuple-element.52.refs_1_, bf16[4,4,128,2048]{3,2,1,0:T(8,128)(2,1)} %get-tuple-element.53.refs_2_, ...), custom_call_target="tpu_custom_call" | custom-call | flops 16220160 | bytes 34603008 | tf_op jit(solution)/shard_map/pallas_call | solution.py:814
  399.4 28.0 %shard_map.291 = (f32[2,704,2048]{2,1,0:T(8,128)}, f32[2,704,2048]{2,1,0:T(8,128)}, f32[2,704,2048]{2,1,0:T(8,128)}) custom-call(bf16[2,1024,2048]{2,1,0:T(8,128)(2,1)} %get-tuple-element.64.rows, bf16[2,1024,2048]{2,1,0:T(8,128)(2,1)} %get-tuple-element.65.pair_grads, bf16[2,1024,704]{2,1,0:T(8,128)(2,1)} %get-tuple-element.66.grad_gate, ...), custom_call_target="tpu_custom_call" | custom-call | flops 17716740096 | bytes 62914560 | tf_op jit(solution)/shard_map/pallas_call | solution.py:1310
  428.4 2.2 copy.149
  430.6 2.2 copy.148
  432.9 2.2 copy.147
  435.7 4.6 convolution_convert_fusion.8
  440.3 2.1 copy.160
  442.4 2.4 fusion.6
  448.9 4.7 fusion.86
  453.6 4.5 convolution_convert_fusion
  461.2 4.6 convolution_convert_fusion.1
  465.8 2.1 convolution_convert_fusion.3
  472.9 3.4 convolution_convert_fusion.2
  476.4 4.4 copy.143
  480.7 3.3 fusion.13
  484.1 3.0 concatenate.73
  487.1 2.0 copy.159
  489.0 1.9 pad.21.clone
  491.0 125.2 %shard_map.290 = (f32[128,1024]{1,0:T(8,128)}, f32[128,1536]{1,0:T(8,128)}, f32[32,2048]{1,0:T(8,128)}, f32[64,576]{1,0:T(8,128)}, f32[64,128]{1,0:T(8,128)}) custom-call(bf16[16,128,1024]{2,1,0:T(8,128)(2,1)} %bitcast.71, bf16[16,128,1536]{2,1,0:T(8,128)(2,1)} %bitcast.70, bf16[16,32,2048]{2,1,0:T(8,128)(2,1)} %bitcast.73, ...), custom_call_target="tpu_custom_call" | custom-call | flops 13148160 | bytes 28049408 | tf_op jit(solution)/shard_map/pallas_call | solution.py:814
  616.2 1.8 fusion.80
  620.1 3.9 fusion.12
  (239 shorter events, 51.4 us)
Async XLA Ops:
  0.6 9.5 %copy-start = (bf16[2048,576]{0,1:T(8,128)(2,1)S(1)}, bf16[2048,576]{0,1:T(8,128)(2,1)}, u32[]{:S(2)}) copy-start(bf16[2048,576]{0,1:T(8,128)(2,1)} %param.20) | copy-start | bytes 7077892
  0.7 8.8 %copy-start.1 = (bf16[128,2048]{1,0:T(8,128)(2,1)S(1)}, bf16[128,2048]{1,0:T(8,128)(2,1)}, u32[]{:S(2)}) copy-start(bf16[128,2048]{1,0:T(8,128)(2,1)} %param.17) | copy-start | bytes 1572868
  0.7 8.8 %copy-start.43 = (f32[2048]{0:T(1024)S(1)}, f32[2048]{0:T(1024)}, u32[]{:S(2)}) copy-start(f32[2048]{0:T(1024)} %param.18) | copy-start | bytes 24580
  3.8 23.3 %collective-permute-start.3 = (bf16[128,2176]{1,0:T(8,128)(2,1)}, bf16[128,2176]{1,0:T(8,128)(2,1)}, u32[]{:S(2)}, u32[]{:S(2)}) collective-permute-start(bf16[128,2176]{1,0:T(8,128)(2,1)} %get-tuple-element.174), channel_id=1, source_target_pairs={{0,4},{2,6},{4,0},{6,2},{8,12},{10,14},{12,8},{14,10},{16,20},{18,... | collective-permute-start | bytes 1671176 | tf_op jit(solution)/shard_map/ppermute | solution.py:437
  6.7 20.3 %collective-permute-start.2 = (bf16[128,2176]{1,0:T(8,128)(2,1)}, bf16[128,2176]{1,0:T(8,128)(2,1)}, u32[]{:S(2)}, u32[]{:S(2)}) collective-permute-start(bf16[128,2176]{1,0:T(8,128)(2,1)} %get-tuple-element.174), channel_id=1, source_target_pairs={{0,2},{2,0},{4,6},{6,4},{8,10},{10,8},{12,14},{14,12},{16,18},{18,... | collective-permute-start | bytes 1671176 | tf_op jit(solution)/shard_map/ppermute | solution.py:433
  10.1 15.8 %copy-start.6 = (bf16[128,2048]{1,0:T(8,128)(2,1)}, bf16[128,2048]{1,0:T(8,128)(2,1)S(1)}, u32[]{:S(2)}) copy-start(bf16[128,2048]{1,0:T(8,128)(2,1)S(1)} %fusion.8) | copy-start | bytes 1572868
  10.1 15.8 %collective-permute-start.1 = (bf16[128,2048]{1,0:T(8,128)(2,1)S(1)}, bf16[128,2048]{1,0:T(8,128)(2,1)}, u32[]{:S(2)}, u32[]{:S(2)}) collective-permute-start(bf16[128,2048]{1,0:T(8,128)(2,1)S(1)} %fusion.8), channel_id=1, source_target_pairs={{0,1},{1,0},{2,3},{3,2},{4,5},{5,4},{6,7},{7,6},{8,9},{9,8},{10,11... | collective-permute-start | bytes 1572872 | tf_op jit(solution)/shard_map/ppermute | solution.py:423
  10.1 3.6 copy-start.56
  10.9 10.8 %copy-start.9 = (f32[128,576]{0,1:T(8,128)}, f32[128,576]{0,1:T(8,128)S(1)}, u32[]{:S(2)}) copy-start(f32[128,576]{0,1:T(8,128)S(1)} %fusion.83) | copy-start | bytes 884740
  12.0 5.7 collective-permute-start
  13.9 20.0 %copy-start.31 = (f32[256,32]{0,1:T(8,128)}, f32[256,32]{0,1:T(8,128)S(1)}, u32[]{:S(2)}) copy-start(f32[256,32]{0,1:T(8,128)S(1)} %get-tuple-element.189) | copy-start | bytes 98308
  13.9 20.0 %copy-start.33 = (f32[256,32]{0,1:T(8,128)}, f32[256,32]{0,1:T(8,128)S(1)}, u32[]{:S(2)}) copy-start(f32[256,32]{0,1:T(8,128)S(1)} %get-tuple-element.190) | copy-start | bytes 98308
  27.0 6.1 copy-start.7
  27.1 14.9 %collective-permute-start.4 = (bf16[128,2176]{1,0:T(8,128)(2,1)}, bf16[128,2176]{1,0:T(8,128)(2,1)}, u32[]{:S(2)}, u32[]{:S(2)}) collective-permute-start(bf16[128,2176]{1,0:T(8,128)(2,1)} %collective-permute-done.2.refs_0_), channel_id=1, source_target_pairs={{0,4},{2,6},{4,0},{6,2},{8,12},{10,14},{12,8},{14,10},{16,20},{18,... | collective-permute-start | bytes 1671176 | tf_op jit(solution)/shard_map/ppermute | solution.py:437
  34.7 4.4 copy-start.40
  35.4 3.7 copy-start.13
  43.4 2.0 collective-permute-start.5
  396.9 38.8 %collective-permute-start.6 = (bf16[128,2048]{1,0:T(8,128)(2,1)}, bf16[128,2048]{1,0:T(8,128)(2,1)}, u32[]{:S(2)}, u32[]{:S(2)}) collective-permute-start(bf16[128,2048]{1,0:T(8,128)(2,1)} %fusion.76), channel_id=1, source_target_pairs={{0,1},{1,0},{2,3},{3,2},{4,5},{5,4},{6,7},{7,6},{8,9},{9,8},{10,11... | collective-permute-start | bytes 1572872 | tf_op jit(solution)/shard_map/ppermute | solution.py:423
  399.4 28.1 %copy-start.5 = (bf16[128,2048]{1,0:T(8,128)(2,1)S(1)}, bf16[128,2048]{1,0:T(8,128)(2,1)}, u32[]{:S(2)}) copy-start(bf16[128,2048]{1,0:T(8,128)(2,1)} %copy-done.4) | copy-start | bytes 1572868
  435.7 6.7 %copy-start.50 = (f32[8,256]{1,0:T(8,128)S(1)}, f32[8,256]{1,0:T(8,128)}, u32[]{:S(2)}) copy-start(f32[8,256]{1,0:T(8,128)} %copy-done.49) | copy-start | bytes 24580
  448.9 4.7 copy-start.8
  453.6 14.2 %copy-start.20 = (f32[256,2048]{1,0:T(8,128)}, f32[256,2048]{1,0:T(8,128)S(1)}, u32[]{:S(2)}) copy-start(f32[256,2048]{1,0:T(8,128)S(1)} %fusion.86) | copy-start | bytes 6291460
  460.5 5.3 copy-start.16
  460.5 8.4 %collective-permute-start.8 = (bf16[128,576]{0,1:T(8,128)(2,1)S(1)}, bf16[128,576]{0,1:T(8,128)(2,1)S(1)}, u32[]{:S(2)}, u32[]{:S(2)}) collective-permute-start(bf16[128,576]{0,1:T(8,128)(2,1)S(1)} %fusion.29), channel_id=1, source_target_pairs={{0,1},{1,0},{2,3},{3,2},{4,5},{5,4},{6,7},{7,6},{8,9},{9,8},{10,11... | collective-permute-start | bytes 442376 | tf_op jit(solution)/shard_map/ppermute | solution.py:423
  468.7 12.0 %collective-permute-start.7 = (bf16[128,2048]{1,0:T(8,128)(2,1)}, bf16[128,2048]{1,0:T(8,128)(2,1)}, u32[]{:S(2)}, u32[]{:S(2)}) collective-permute-start(bf16[128,2048]{1,0:T(8,128)(2,1)} %slice.273), channel_id=1, source_target_pairs={{0,1},{1,0},{2,3},{3,2},{4,5},{5,4},{6,7},{7,6},{8,9},{9,8},{10,11... | collective-permute-start | bytes 1572872 | tf_op jit(solution)/shard_map/ppermute | solution.py:423
  476.4 4.4 copy-start.44
  490.9 129.1 %copy-start.39 = (f32[2048]{0:T(1024)S(1)}, f32[2048]{0:T(1024)}, u32[]{:S(2)}) copy-start(f32[2048]{0:T(1024)} %param.24) | copy-start | bytes 24580
  490.9 129.1 %copy-start.53 = (f32[128]{0:T(128)S(1)}, f32[128]{0:T(128)}, u32[]{:S(2)}) copy-start(f32[128]{0:T(128)} %copy-done.51) | copy-start | bytes 1540
  491.0 129.1 %copy-start.55 = (f32[128]{0:T(128)S(1)}, f32[128]{0:T(128)}, u32[]{:S(2)}) copy-start(f32[128]{0:T(128)} %copy-done.54) | copy-start | bytes 1540
  491.0 129.1 %copy-start.61 = (f32[128]{0:T(128)S(1)}, f32[128]{0:T(128)}, u32[]{:S(2)}) copy-start(f32[128]{0:T(128)} %copy-done.60) | copy-start | bytes 1540
  620.1 3.9 copy-start.22
  620.1 4.8 copy-start.36
  (44 other events, 81.4 us)
